TPU v7x, 128 devices: a whole 4x4x4 slice. The times are simulated.
128 devices in a mesh: row: 8 (over y, core), col: 16 (over x, z).
Axes of the slice: x: 4, y: 4, z: 4, core: 2. Of those that a mesh axis runs over, the one named last changes fastest.
Arguments:
- grad: bfloat16 [8192, 4096], P('row', 'col'), may hold values from -6 to 6
- basis_left: bfloat16 [8192, 8192], P('row', 'col'), may hold values from -0.0625 to 0.0625
- basis_right: bfloat16 [4096, 4096], P('row', 'col'), may hold values from -0.09375 to 0.09375
- first_moment: float32 [8192, 4096], P('col', 'row'), may hold values from -6 to 6
- second_moment: float32 [8192, 4096], P('col', 'row'), may hold values from 0.25 to 4
Outputs:
- update: bfloat16 [8192, 4096], P('row', 'col')
- first_new: float32 [8192, 4096], P('col', 'row')
- second_new: float32 [8192, 4096], P('col', 'row')
All inputs are finite; a program needn't handle non-finite values.
Results may differ from a plain program's by a relative error of at most 0.029.
Values may be sent and summed in bfloat16 or wider, within the bound.
A program may use at most 64 MiB of HBM per device.

v0:
```python
import jax
import jax.numpy as jnp
from jax import lax
from jax.sharding import PartitionSpec as P


def rotate_forward(left_matrix, contract_dim, moving_matrix):

    def product(pieces, offset):
        return lax.dot_general(
            left_matrix,
            pieces,
            (((contract_dim,), (0,)), ((), ())),
            preferred_element_type=jnp.float32,
        )

    partial_terms = product(lax.all_gather(moving_matrix, "col", axis=1, tiled=True), jnp.int32(0))
    return lax.psum_scatter(
        partial_terms.astype(jnp.bfloat16), "row", scatter_dimension=1, tiled=True
    ).astype(jnp.float32)


def rotate_backward(left_matrix, moving_matrix):

    def product(pieces, offset):
        return lax.dot_general(
            left_matrix, pieces, (((1,), (1,)), ((), ())), preferred_element_type=jnp.float32
        )

    partial_terms = product(lax.all_gather(moving_matrix, "row", axis=0, tiled=True), jnp.int32(0))
    return lax.psum_scatter(
        partial_terms.astype(jnp.bfloat16), "col", scatter_dimension=1, tiled=True
    )


def per_device(grad, basis_left, basis_right, first_moment, second_moment):
    left_rotated = rotate_forward(basis_left, 0, grad).astype(jnp.bfloat16)
    rotated = rotate_forward(left_rotated, 1, basis_right)
    first_new = 0.9 * first_moment + 0.1 * rotated
    second_new = 0.95 * second_moment + 0.05 * rotated * rotated
    direction = (first_new / (jnp.sqrt(second_new) + 1e-08)).astype(jnp.bfloat16)
    back_left = rotate_backward(basis_left, direction.T)
    update = rotate_backward(back_left, basis_right)
    return (update, first_new, second_new)


def solution(mesh):
    in_specs = (P("row", "col"), P("row", "col"), P("row", "col"), P("col", "row"), P("col", "row"))
    out_specs = (P("row", "col"), P("col", "row"), P("col", "row"))
    return jax.shard_map(
        per_device, mesh=mesh, in_specs=in_specs, out_specs=out_specs, check_vma=False
    )
```

profile of v0, /device:TPU:0, one launch (start us, length us, event | category | flops | bytes accessed | tf_op | source)
XLA Modules:
  0.0 481.6 jit_solution(10201881834202111614)
XLA Ops:
  7.2 0.0 copy-start
  7.2 0.0 all-gather.5.cloned.1.call-start
  7.2 0.7 all-gather.5.cloned.1.call-update
  7.9 0.0 all-gather.7.cloned.1.call-start
  8.0 0.7 all-gather.7.cloned.1.call-update
  8.7 0.0 reduce-scatter.5.cloned.1.call-start
  8.7 82.4 %all-gather.5.cloned.1.call-done = bf16[1024,4096]{1,0:T(8,128)(2,1)} async-done(((bf16[1024,256]{1,0:T(8,128)(2,1)}), bf16[1024,4096]{1,0:T(8,128)(2,1)}) %all-gather.5.cloned.1.call-update) | async-done | bytes 8388624 | tf_op jit(solution)/shard_map/all_gather | solution.py:17
  91.1 0.0 copy-done
  91.1 9.5 %convolution_convert_fusion.1 = bf16[512,4096]{1,0:T(8,128)(2,1)} fusion(bf16[1024,512]{1,0:T(8,128)(2,1)S(1)} %copy-done, bf16[1024,4096]{1,0:T(8,128)(2,1)} %all-gather.5.cloned.1.call-done), kind=kOutput, calls=%fused_computation.2 | convolution fusion | flops 4297064448 | bytes 13631488 | tf_op jit(solution)/shard_map/dot_general | solution.py:10
  100.6 0.0 reduce-scatter.5.cloned.1.call-update
  100.6 0.0 reduce-scatter.7.cloned.1.call-start
  100.7 49.6 %all-gather.7.cloned.1.call-done = bf16[512,4096]{1,0:T(8,128)(2,1)} async-done(((bf16[512,256]{1,0:T(8,128)(2,1)}), bf16[512,4096]{1,0:T(8,128)(2,1)}) %all-gather.7.cloned.1.call-update) | async-done | bytes 4194320 | tf_op jit(solution)/shard_map/all_gather | solution.py:17
  150.2 39.6 %reduce-scatter.5.cloned.1.call-done = bf16[512,512]{1,0:T(8,128)(2,1)} async-done(((bf16[512,4096]{1,0:T(8,128)(2,1)}), bf16[512,512]{1,0:T(8,128)(2,1)}) %reduce-scatter.5.cloned.1.call-update) | async-done | bytes 524304 | tf_op jit(solution)/shard_map/reduce_scatter | solution.py:18
  189.8 6.7 %convolution_convert_fusion.2 = bf16[512,4096]{1,0:T(8,128)(2,1)} fusion(bf16[512,512]{1,0:T(8,128)(2,1)} %reduce-scatter.5.cloned.1.call-done, bf16[512,4096]{1,0:T(8,128)(2,1)} %all-gather.7.cloned.1.call-done), kind=kOutput, calls=%fused_computation.3 | convolution fusion | flops 2149580800 | bytes 8912896 | tf_op jit(solution)/shard_map/dot_general | solution.py:10
  196.5 0.0 copy-start.1
  196.5 0.0 copy-start.2
  196.5 0.0 reduce-scatter.7.cloned.1.call-update
  196.5 0.0 all-gather.9.cloned.1.call-start
  196.6 36.8 %reduce-scatter.7.cloned.1.call-done = bf16[512,512]{1,0:T(8,128)(2,1)} async-done(((bf16[512,4096]{1,0:T(8,128)(2,1)}), bf16[512,512]{1,0:T(8,128)(2,1)}) %reduce-scatter.7.cloned.1.call-update) | async-done | bytes 524304 | tf_op jit(solution)/shard_map/reduce_scatter | solution.py:18
  233.4 0.0 copy-done.1
  233.4 0.0 copy-done.2
  233.4 2.9 fusion.2
  236.3 0.0 all-gather.9.cloned.1.call-update
  236.3 0.0 all-gather.11.cloned.1.call-start
  236.4 0.5 all-gather.11.cloned.1.call-update
  236.9 0.0 reduce-scatter.9.cloned.1.call-start
  236.9 30.5 %all-gather.9.cloned.1.call-done = bf16[4096,512]{0,1:T(8,128)(2,1)} async-done(((bf16[512,512]{0,1:T(8,128)(2,1)}), bf16[4096,512]{0,1:T(8,128)(2,1)}) %all-gather.9.cloned.1.call-update) | async-done | bytes 4194320 | tf_op jit(solution)/shard_map/all_gather | solution.py:30
  267.4 9.1 %convert_bitcast_fusion = bf16[1024,4096]{0,1:T(8,128)(2,1)} fusion(bf16[4096,512]{0,1:T(8,128)(2,1)} %all-gather.9.cloned.1.call-done, bf16[1024,512]{1,0:T(8,128)(2,1)S(1)} %copy-done), kind=kOutput, calls=%fused_computation | convolution fusion | flops 4299161600 | bytes 13631488 | tf_op jit(solution)/shard_map/dot_general | solution.py:26
  276.5 0.0 reduce-scatter.9.cloned.1.call-update
  276.5 0.0 reduce-scatter.11.cloned.1.call-start
  276.6 17.6 %all-gather.11.cloned.1.call-done = bf16[4096,256]{1,0:T(8,128)(2,1)} async-done(((bf16[512,256]{1,0:T(8,128)(2,1)}), bf16[4096,256]{1,0:T(8,128)(2,1)}) %all-gather.11.cloned.1.call-update) | async-done | bytes 2097168 | tf_op jit(solution)/shard_map/all_gather | solution.py:30
  294.1 88.9 %reduce-scatter.9.cloned.1.call-done = bf16[1024,256]{0,1:T(8,128)(2,1)} async-done(((bf16[1024,4096]{0,1:T(8,128)(2,1)}), bf16[1024,256]{0,1:T(8,128)(2,1)}) %reduce-scatter.9.cloned.1.call-update) | async-done | bytes 524304 | tf_op jit(solution)/shard_map/reduce_scatter | solution.py:31
  383.1 7.4 %convolution_convert_fusion = bf16[1024,4096]{1,0:T(8,128)(2,1)} fusion(bf16[1024,256]{0,1:T(8,128)(2,1)} %reduce-scatter.9.cloned.1.call-done, bf16[4096,256]{1,0:T(8,128)(2,1)} %all-gather.11.cloned.1.call-done), kind=kOutput, calls=%fused_computation.1 | convolution fusion | flops 2151677952 | bytes 11010048 | tf_op jit(solution)/shard_map/dot_general | solution.py:26
  390.5 0.0 reduce-scatter.11.cloned.1.call-update
  390.5 84.3 %reduce-scatter.11.cloned.1.call-done = bf16[1024,256]{1,0:T(8,128)(2,1)} async-done(((bf16[1024,4096]{1,0:T(8,128)(2,1)}), bf16[1024,256]{1,0:T(8,128)(2,1)}) %reduce-scatter.11.cloned.1.call-update) | async-done | bytes 524304 | tf_op jit(solution)/shard_map/reduce_scatter | solution.py:31
Async XLA Ops:
  7.2 84.0 %copy-start = (bf16[1024,512]{1,0:T(8,128)(2,1)S(1)}, bf16[1024,512]{1,0:T(8,128)(2,1)}, u32[]{:S(2)}) copy-start(bf16[1024,512]{1,0:T(8,128)(2,1)} %param.6) | copy-start | bytes 3145732
  7.2 83.9 %all-gather.5.cloned.1.call-start = ((), (), s32[]{:S(2)}) async-start(), calls=%async_computation.4 | async-start | bytes 8912896 | tf_op jit(solution)/shard_map/all_gather | solution.py:17
  7.9 142.3 %all-gather.7.cloned.1.call-start = ((), (), s32[]{:S(2)}) async-start(), calls=%async_computation.6 | async-start | bytes 4456448 | tf_op jit(solution)/shard_map/all_gather | solution.py:17
  8.7 181.2 %reduce-scatter.5.cloned.1.call-start = ((), (), s32[]{:S(2)}) async-start(), calls=%async_computation.5 | async-start | bytes 4718592 | tf_op jit(solution)/shard_map/reduce_scatter | solution.py:18
  100.6 132.8 %reduce-scatter.7.cloned.1.call-start = ((), (), s32[]{:S(2)}) async-start(), calls=%async_computation.7 | async-start | bytes 4718592 | tf_op jit(solution)/shard_map/reduce_scatter | solution.py:18
  196.5 36.9 %copy-start.1 = (f32[512,512]{1,0:T(8,128)S(1)}, f32[512,512]{1,0:T(8,128)}, u32[]{:S(2)}) copy-start(f32[512,512]{1,0:T(8,128)} %param.9) | copy-start | bytes 3145732
  196.5 36.9 %copy-start.2 = (f32[512,512]{1,0:T(8,128)S(1)}, f32[512,512]{1,0:T(8,128)}, u32[]{:S(2)}) copy-start(f32[512,512]{1,0:T(8,128)} %param.8) | copy-start | bytes 3145732
  196.5 70.9 %all-gather.9.cloned.1.call-start = ((), (), s32[]{:S(2)}) async-start(), calls=%async_computation.8 | async-start | bytes 4718592 | tf_op jit(solution)/shard_map/all_gather | solution.py:30
  236.3 57.8 %all-gather.11.cloned.1.call-start = ((), (), s32[]{:S(2)}) async-start(), calls=%async_computation.10 | async-start | bytes 2359296 | tf_op jit(solution)/shard_map/all_gather | solution.py:30
  236.9 146.2 %reduce-scatter.9.cloned.1.call-start = ((), (), s32[]{:S(2)}) async-start(), calls=%async_computation.9 | async-start | bytes 8912896 | tf_op jit(solution)/shard_map/reduce_scatter | solution.py:31
  276.5 198.2 %reduce-scatter.11.cloned.1.call-start = ((), (), s32[]{:S(2)}) async-start(), calls=%async_computation.11 | async-start | bytes 8912896 | tf_op jit(solution)/shard_map/reduce_scatter | solution.py:31
Sparse Core Ops, SparseCore 0:
  10.1 80.9 all-gather.4
  93.2 56.9 all-gather.6
  152.6 37.1 reduce-scatter.4
  196.6 36.7 reduce-scatter.6
  236.4 30.9 all-gather.8
  269.0 25.1 all-gather.10
  297.5 85.4 reduce-scatter.8
  390.6 84.0 reduce-scatter.10
where the time goes:
time: 482 us
  waiting for transfers between devices  432 us (90%)
  matrix products  32.6 us (7%)
  between operations  14.1 us (3%)
    reduce_scatter x2, waiting for transfers between devices, rotate_backward(): lax.psum_scatter(partial_terms.astype(jnp.bfloat16), 'col', scatter_dimen...  173 us
    all_gather x2, waiting for transfers between devices, rotate_forward(): lax.all_gather(moving_matrix, 'col', axis=1, tiled=True)  132 us
    reduce_scatter x2, waiting for transfers between devices, rotate_forward(): lax.psum_scatter(partial_terms.astype(jnp.bfloat16), 'row', scatter_dimen...  76.4 us
    all_gather x2, waiting for transfers between devices, rotate_backward(): lax.all_gather(moving_matrix, 'row', axis=0, tiled=True)  48 us
    dot_general x2, matrix products, product(): lax.dot_general(left_matrix, pieces, (((1,), (1,)), ((), ())), preferred_...  16.5 us
    dot_general x2, matrix products, product(): lax.dot_general(left_matrix, pieces, (((contract_dim,), (0,)), ((), ())),...  16.1 us
  transfers between devices with their start and end apart: 8, of which 8 were waited for; matrix products, arithmetic and copies ran while one was open for 4% of the time, Pallas kernels for 0%

commit v1 on v0

v1 whole, which is shorter than its diff:
```python
import functools

import jax
import jax.numpy as jnp
from jax import lax
from jax.experimental import pallas as pl
from jax.experimental.pallas import tpu as pltpu
from jax.sharding import PartitionSpec as P

MESH = pl.DeviceIdType.MESH
BF = jnp.bfloat16
F32 = jnp.float32
NK = 2
NM = 2
KC = 1024 // NK
MC = 1024 // NM
MT = MC // 4
OPS = ("g", "trs", "tag", "rrs", "dag", "brs", "bag", "urs")


def wrap(v):
    return lax.rem(v + 8, 4)


def kernel(
    g_ref, l_ref, r_ref, fm_ref, sm_ref,
    u_ref, fn_ref, sn_ref,
    gx, rb, tp, t_own, tx, lh, pp, qq, rot_own, rot_home, d_home, d_own, dall, blp, bl_own, blz, up,
    t_comb, t_fin, r_comb, r_fin, b_comb, b_fin, u_comb, u_fin,
    ring_s, ring_r, l_s, l_r, ra_s, ra_r, r1_s, r1_r, rsib_s, rsib_r, psib_s, psib_r,
    fwd_s, fwd_r, back_s, back_r, dsib_s, dsib_r,
):
    row, col = lax.axis_index("row"), lax.axis_index("col")
    y, c, x, z = row // 2, lax.rem(row, 2), col // 4, lax.rem(col, 4)
    other = 1 - c

    def dev(x, y, z, c):
        return (y * 2 + c, x * 4 + z)

    sib = dev(x, y, z, other)
    ring = {
        "x": (x, dev(wrap(x + 1), y, z, c), dev(wrap(x - 1), y, z, c)),
        "y": (y, dev(x, wrap(y + 1), z, c), dev(x, wrap(y - 1), z, c)),
        "z": (z, dev(x, y, wrap(z + 1), c), dev(x, y, wrap(z - 1), c)),
    }

    barrier = pltpu.get_barrier_semaphore()
    partners = [ring["x"][1], ring["x"][2], ring["y"][1], ring["y"][2], sib]
    for d in (1, 2, 3):
        partners += [dev(x, y, wrap(z + d), c), dev(x, y, wrap(z + d), other)]
    for partner in partners:
        pl.semaphore_signal(barrier, inc=1, device_id=partner, device_id_type=MESH)
    pl.semaphore_wait(barrier, len(partners))

    sent = []

    def send(src, dst, ssem, rsem, device):
        copy = pltpu.make_async_remote_copy(
            src_ref=src, dst_ref=dst, send_sem=ssem, recv_sem=rsem, device_id=device, device_id_type=MESH
        )
        copy.start()
        sent.append((None, copy))

    def arrived(dst, ssem, rsem):
        pltpu.make_async_remote_copy(
            src_ref=dst, dst_ref=dst, send_sem=ssem, recv_sem=rsem, device_id=sib, device_id_type=MESH
        ).wait_recv()

    def send_or_keep(mine, src, dst, ssem, rsem, device):
        copy = pltpu.make_async_remote_copy(
            src_ref=src, dst_ref=dst, send_sem=ssem, recv_sem=rsem, device_id=device, device_id_type=MESH
        )

        @pl.when(jnp.logical_not(mine))
        def _():
            copy.start()

        @pl.when(mine)
        def _():
            dst[...] = src[...]

        sent.append((mine, copy))

    def arrived_or_kept(mine, dst, ssem, rsem):
        @pl.when(jnp.logical_not(mine))
        def _():
            arrived(dst, ssem, rsem)

    class Ring:
        def __init__(self, axis, ssem, rsem, half):
            self.pos, self.right_dev, self.left_dev = ring[axis]
            self.right, self.left, self.opp = wrap(self.pos + 1), wrap(self.pos - 1), wrap(self.pos + 2)
            self.ssem, self.rsem, self.half = ssem, rsem, half

        def go(self, j, n, src, dst):
            send(src, dst, self.ssem(j, n), self.rsem(j, n), self.right_dev if n < 3 else self.left_dev)

        def wait(self, j, n, dst):
            arrived(dst, self.ssem(j, n), self.rsem(j, n))

        def rows(self, j, h):
            return pl.ds((2 * j + h) * self.half, self.half)

    class Gather(Ring):
        def __init__(self, axis, ssem, rsem, half, src, dst):
            super().__init__(axis, ssem, rsem, half)
            self.src, self.dst = src, dst

        def start(self, j, keep=True):
            a, b = self.rows(j, 0), self.rows(j, 1)
            self.go(j, 0, self.src(a), self.dst(self.pos, a))
            self.go(j, 3, self.src(b), self.dst(self.pos, b))
            self.go(j, 1, self.src(b), self.dst(self.pos, b))
            self.go(j, 4, self.src(a), self.dst(self.pos, a))
            if keep:
                for r in (a, b):
                    self.dst(self.pos, r)[...] = self.src(r)[...]

        def mid(self, j):
            a, b = self.rows(j, 0), self.rows(j, 1)
            self.wait(j, 0, self.dst(self.left, a))
            self.go(j, 2, self.dst(self.left, a), self.dst(self.left, a))
            self.wait(j, 3, self.dst(self.right, b))
            self.go(j, 5, self.dst(self.right, b), self.dst(self.right, b))

        def end(self, j):
            a, b = self.rows(j, 0), self.rows(j, 1)
            self.wait(j, 1, self.dst(self.left, b))
            self.wait(j, 4, self.dst(self.right, a))
            self.wait(j, 2, self.dst(self.opp, a))
            self.wait(j, 5, self.dst(self.opp, b))

    class Scatter(Ring):
        def __init__(self, axis, ssem, rsem, half, piece, comb, fin, out):
            super().__init__(axis, ssem, rsem, half)
            self.piece, self.comb, self.fin, self.out = piece, comb, fin, out

        def start(self, j):
            a, b = self.rows(j, 0), self.rows(j, 1)
            self.go(j, 0, self.piece(self.opp, a), self.comb.at[j, 0])
            self.go(j, 3, self.piece(self.opp, b), self.comb.at[j, 1])
            self.go(j, 1, self.piece(self.right, b), self.fin.at[j, 0, 1])
            self.go(j, 4, self.piece(self.left, a), self.fin.at[j, 1, 0])

        def mid(self, j):
            a, b = self.rows(j, 0), self.rows(j, 1)
            for n, side, r, h in ((0, self.right, a, 0), (3, self.left, b, 1)):
                self.wait(j, n, self.comb.at[j, h])
                ref = self.piece(side, r)
                ref[...] = (ref[...].astype(F32) + self.comb[j, h].astype(F32)).astype(BF)
                self.go(j, n + 2, ref, self.fin.at[j, h, h])

        def end(self, j):
            for h, first, second in ((0, 4, 2), (1, 1, 5)):
                r = self.rows(j, h)
                self.wait(j, first, self.fin.at[j, 1 - h, h])
                self.wait(j, second, self.fin.at[j, h, h])
                total = self.piece(self.pos, r)[...].astype(F32)
                total = total + self.fin[j, 0, h].astype(F32) + self.fin[j, 1, h].astype(F32)
                self.out(r)[...] = total.astype(BF)

    def ring_sems(name):
        i = OPS.index(name)
        return (lambda j, n: ring_s.at[i, j, n]), (lambda j, n: ring_r.at[i, j, n])

    def columns(ref, n, width=256):
        return lambda t, r: ref.at[r, pl.ds(pl.multiple_of(t * width, width), width)]

    def pieces(ref):
        return lambda t, r: ref.at[t, r]

    kh, mh = KC // 2, MC // 2
    g_ag = Gather("x", *ring_sems("g"), kh, lambda r: g_ref.at[r], columns(gx, 4))
    t_rs = Scatter("z", *ring_sems("trs"), kh, pieces(tp), t_comb, t_fin, lambda r: t_own.at[r])
    t_ag = Gather("x", *ring_sems("tag"), kh, lambda r: t_own.at[r], pieces(tx))
    r_rs = Scatter("y", *ring_sems("rrs"), mh, lambda t, r: pp.at[c, t, r], r_comb, r_fin, lambda r: rot_own.at[r])
    d_ag = Gather("y", *ring_sems("dag"), mh, lambda r: d_own.at[r], lambda t, r: dall.at[c, t, r])
    b_rs = Scatter("x", *ring_sems("brs"), kh, pieces(blp), b_comb, b_fin, lambda r: bl_own.at[r])
    b_ag = Gather("z", *ring_sems("bag"), kh, lambda r: bl_own.at[r], columns(blz, 4))
    u_rs = Scatter("x", *ring_sems("urs"), kh, pieces(up), u_comb, u_fin, lambda r: u_ref.at[r])

    def l_unit(h, j):
        i = h * NM + j
        return Gather(
            "z",
            lambda _, n: l_s.at[i, n],
            lambda _, n: l_r.at[i, n],
            512,
            lambda r: l_ref.at[r, pl.ds(h * 256 + j * MT, MT)],
            lambda t, r: lh.at[h, r, pl.ds(pl.multiple_of(j * MC + t * MT, MT), MT)],
        )

    l_units = [l_unit(h, j) for j in range(NM) for h in range(2)]

    def rb_block(t, cc):
        return rb.at[pl.ds(pl.multiple_of(t * 256 + cc * 128, 128), 128)]

    def rb_rows(t, r):
        return rb.at[pl.ds(pl.multiple_of(t * 256 + c * 128 + r.start, 64), r.size)]

    r_ag = Gather("y", lambda _, n: ra_s.at[n], lambda _, n: ra_r.at[n], 64, lambda r: rb_rows(y, r), rb_rows)

    def rb_tile(cc, zz):
        return rb.at[
            pl.ds(pl.multiple_of(y * 256 + cc * 128, 128), 128), pl.ds(pl.multiple_of(zz * 256, 256), 256)
        ]

    for sl in range(2):
        for cc in range(2):
            mine = jnp.logical_and(2 * c + sl == z, c == cc)
            send_or_keep(
                mine, r_ref.at[pl.ds(sl * 256 + cc * 128, 128)], rb_tile(cc, z),
                r1_s.at[sl, cc], r1_r.at[z], dev(x, y, 2 * c + sl, cc),
            )
    for j in range(NK):
        g_ag.start(j)
    for unit in l_units:
        unit.start(0)
    for zz in range(4):
        mine = jnp.logical_and(zz == z, z // 2 == c)
        arrived_or_kept(mine, rb_tile(c, zz), r1_s.at[0, 0], r1_r.at[zz])
    r_ag.start(0, keep=False)

    def sib_block(t, n):
        send(rb_block(t, c), rb_block(t, c), rsib_s.at[n], rsib_r.at[n], sib)

    sib_block(y, 0)
    g_ag.mid(0)
    r_ag.mid(0)
    for j in range(1, NK):
        g_ag.mid(j)
    r_ag.end(0)
    for n, t in enumerate((r_ag.left, r_ag.right, r_ag.opp)):
        sib_block(t, n + 1)
    for n, t in enumerate((y, r_ag.left, r_ag.right, r_ag.opp)):
        arrived(rb_block(t, other), rsib_s.at[n], rsib_r.at[n])

    def rotate_right(j):
        rows = pl.ds(j * KC, KC)

        def body(b, _):
            right = rb[:, pl.ds(pl.multiple_of(b * 256, 256), 256)]
            tp[b, rows] = jnp.dot(gx[rows], right, preferred_element_type=F32).astype(BF)
            return 0

        lax.fori_loop(0, 4, body, 0)

    for j in range(NK):
        g_ag.end(j)
        rotate_right(j)
        t_rs.start(j)
    for j in range(NK):
        t_rs.mid(j)
    for unit in l_units:
        unit.mid(0)
    for j in range(NK):
        t_rs.end(j)
        t_ag.start(j)
    for j in range(NK):
        t_ag.mid(j)
    for unit in l_units:
        unit.end(0)
    for j in range(NK):
        t_ag.end(j)

    def rotate_left(h, j):
        rows = pl.ds(j * MC, MC)

        def body(a, _):
            pp[h, a, rows] = lax.dot_general(
                lh[h, :, rows], tx[a], (((0,), (0,)), ((), ())), preferred_element_type=F32
            ).astype(BF)
            return 0

        lax.fori_loop(0, 4, body, 0)

    for j in range(NM):
        rows = pl.ds(j * MC, MC)
        rotate_left(other, j)
        for a in range(4):
            send(pp.at[other, a, rows], qq.at[a, rows], psib_s.at[j, a], psib_r.at[j, a], sib)
        rotate_left(c, j)
    for j in range(NM):
        rows = pl.ds(j * MC, MC)
        for a in range(4):
            arrived(qq.at[a, rows], psib_s.at[j, a], psib_r.at[j, a])
            pp[c, a, rows] = (pp[c, a, rows].astype(F32) + qq[a, rows].astype(F32)).astype(BF)
        r_rs.start(j)
    for j in range(NM):
        r_rs.mid(j)

    def home_tile(ref, cc, s, j):
        return ref.at[
            pl.ds(pl.multiple_of(cc * 256 + j * MT, MT), MT), pl.ds(pl.multiple_of(s * 256, 256), 256)
        ]

    def own_tile(ref, zz, j):
        return ref.at[pl.ds(pl.multiple_of(j * MC + zz * MT, MT), MT)]

    for j in range(NM):
        r_rs.end(j)
        for d in range(4):
            zz = wrap(z + d)
            place = (own_tile(rot_own, zz, j), home_tile(rot_home, c, lax.rem(z, 2), j),
                     fwd_s.at[j, d], fwd_r.at[j, lax.rem(z, 2) * 2 + c], dev(x, y, zz, z // 2))
            if d:
                send(*place)
            else:
                send_or_keep(z // 2 == c, *place)
    for j in range(NM):
        for s in range(2):
            for cc in range(2):
                mine = jnp.logical_and(2 * c + s == z, c == cc)
                arrived_or_kept(mine, home_tile(rot_home, cc, s, j), fwd_s.at[j, 0], fwd_r.at[j, s * 2 + cc])
        for h in range(2):
            rows = pl.ds(h * 256 + j * MT, MT)
            rotated = rot_home[rows].astype(F32)
            first = 0.9 * fm_ref[rows] + 0.1 * rotated
            second = 0.95 * sm_ref[rows] + 0.05 * rotated * rotated
            fn_ref[rows] = first
            sn_ref[rows] = second
            d_home[rows] = (first / (jnp.sqrt(second) + 1e-08)).astype(BF)
        for h in range(2):
            for s in range(2):
                mine = jnp.logical_and(2 * c + s == z, c == h)
                send_or_keep(
                    mine, home_tile(d_home, h, s, j), own_tile(d_own, z, j),
                    back_s.at[j, h, s], back_r.at[j, z], dev(x, y, 2 * c + s, h),
                )
    for j in range(NM):
        for zz in range(4):
            mine = jnp.logical_and(zz == z, z // 2 == c)
            arrived_or_kept(mine, own_tile(d_own, zz, j), back_s.at[j, 0, 0], back_r.at[j, zz])
        d_ag.start(j)

    def d_block(t, j, cc):
        return dall.at[cc, t, pl.ds(j * MC, MC)]

    order = (y, d_ag.left, d_ag.right, d_ag.opp)
    for j in range(NM):
        send(d_block(y, j, c), d_block(y, j, c), dsib_s.at[j, 0], dsib_r.at[j, 0], sib)
        d_ag.mid(j)
    for j in range(NM):
        d_ag.end(j)
        for n in (1, 2, 3):
            send(d_block(order[n], j, c), d_block(order[n], j, c), dsib_s.at[j, n], dsib_r.at[j, n], sib)
    for j in range(NM):
        for n in range(4):
            arrived(d_block(order[n], j, other), dsib_s.at[j, n], dsib_r.at[j, n])

    def rotate_back_left(j):
        rows = pl.ds(j * KC, KC)

        def body(a, _):
            total = jnp.dot(lh[0, rows], dall[0, a], preferred_element_type=F32)
            total = total + jnp.dot(lh[1, rows], dall[1, a], preferred_element_type=F32)
            blp[a, rows] = total.astype(BF)
            return 0

        lax.fori_loop(0, 4, body, 0)

    def rotate_back_right(j):
        rows = pl.ds(j * KC, KC)

        def body(t, _):
            right = rb[pl.ds(pl.multiple_of(t * 256, 256), 256)]
            up[t, rows] = lax.dot_general(
                blz[rows], right, (((1,), (1,)), ((), ())), preferred_element_type=F32
            ).astype(BF)
            return 0

        lax.fori_loop(0, 4, body, 0)

    for j in range(NK):
        rotate_back_left(j)
        b_rs.start(j)
    for j in range(NK):
        b_rs.mid(j)
    for j in range(NK):
        b_rs.end(j)
        b_ag.start(j)
    for j in range(NK):
        b_ag.mid(j)
    for j in range(NK):
        b_ag.end(j)
        rotate_back_right(j)
        u_rs.start(j)
    for j in range(NK):
        u_rs.mid(j)
    for j in range(NK):
        u_rs.end(j)

    for mine, copy in sent:
        if mine is None:
            copy.wait_send()
        else:
            @pl.when(jnp.logical_not(mine))
            def _(copy=copy):
                copy.wait_send()


def per_device(grad, basis_left, basis_right, first_moment, second_moment):
    dma = pltpu.SemaphoreType.DMA
    kh, mh = KC // 2, MC // 2

    def scatter_buffers(chunks, half):
        return [pltpu.VMEM((chunks, 2, half, 256), BF), pltpu.VMEM((chunks, 2, 2, half, 256), BF)]

    scratch = [
        pltpu.VMEM((1024, 1024), BF),
        pltpu.VMEM((1024, 1024), BF),
        pltpu.VMEM((4, 1024, 256), BF),
        pltpu.VMEM((1024, 256), BF),
        pltpu.VMEM((4, 1024, 256), BF),
        pltpu.VMEM((2, 1024, 1024), BF),
        pltpu.VMEM((2, 4, 1024, 256), BF),
        pltpu.VMEM((4, 1024, 256), BF),
        pltpu.VMEM((1024, 256), BF),
        pltpu.VMEM((512, 512), BF),
        pltpu.VMEM((512, 512), BF),
        pltpu.VMEM((1024, 256), BF),
        pltpu.VMEM((2, 4, 1024, 256), BF),
        pltpu.VMEM((4, 1024, 256), BF),
        pltpu.VMEM((1024, 256), BF),
        pltpu.VMEM((1024, 1024), BF),
        pltpu.VMEM((4, 1024, 256), BF),
    ]
    scratch += scatter_buffers(NK, kh) + scatter_buffers(NM, mh) + scatter_buffers(NK, kh) + scatter_buffers(NK, kh)
    most = max(NK, NM)
    for out, back in (
        ((len(OPS), most, 6), (len(OPS), most, 6)), ((2 * NM, 6), (2 * NM, 6)), ((6,), (6,)), ((2, 2), (4,)),
        ((4,), (4,)), ((NM, 4), (NM, 4)), ((NM, 4), (NM, 4)), ((NM, 2, 2), (NM, 4)), ((NM, 4), (NM, 4)),
    ):
        scratch += [dma(out), dma(back)]
    vmem = pl.BlockSpec(memory_space=pltpu.VMEM)
    return pl.pallas_call(
        kernel,
        out_shape=(
            jax.ShapeDtypeStruct((1024, 256), BF),
            jax.ShapeDtypeStruct((512, 512), F32),
            jax.ShapeDtypeStruct((512, 512), F32),
        ),
        in_specs=[vmem] * 5,
        out_specs=[vmem] * 3,
        scratch_shapes=scratch,
        compiler_params=pltpu.CompilerParams(
            collective_id=0, has_side_effects=True, vmem_limit_bytes=60 * 1024 * 1024
        ),
        cost_estimate=pl.CostEstimate(flops=12884901888, bytes_accessed=6553600, transcendentals=262144),
    )(grad, basis_left, basis_right, first_moment, second_moment)


def solution(mesh):
    in_specs = (P("row", "col"), P("row", "col"), P("row", "col"), P("col", "row"), P("col", "row"))
    out_specs = (P("row", "col"), P("col", "row"), P("col", "row"))
    return jax.shard_map(
        per_device, mesh=mesh, in_specs=in_specs, out_specs=out_specs, check_vma=False
    )
```

time: 482 us -> 192 us (0.40)
  waiting for transfers between devices: 432 us -> 0 us
  Pallas kernels: 0 us -> 186 us
  matrix products: 32.6 us -> 0 us
  between operations: 14.1 us -> 0.65 us
    reduce_scatter x4 -> x0, waiting for transfers between devices: 250 us -> none  [the longest x2 173 us: rotate_backward(): lax.psum_scatter(partial_terms.astype(jnp.bfloat16), 'col', scatter_dimen...]
    pallas_call x0 -> x1, Pallas kernels: none -> 186 us  [per_device(): pl.pallas_call(kernel, out_shape=(jax.ShapeDtypeStruct((1024, 256), BF),...]
    all_gather x4 -> x0, waiting for transfers between devices: 180 us -> none  [the longest x2 132 us: rotate_forward(): lax.all_gather(moving_matrix, 'col', axis=1, tiled=True)]
    dot_general x4 -> x0, matrix products: 32.6 us -> none  [the longest x2 16.5 us: product(): lax.dot_general(left_matrix, pieces, (((1,), (1,)), ((), ())), preferred_...]
  transfers between devices with their start and end apart: 8 -> 0, of which waited for: 8 -> 0; matrix products, arithmetic and copies ran while one was open for 4% -> 0% of each run, Pallas kernels for 0% -> 0%
where the time goes in v1:
time: 192 us; the launch traced here: 191 us
  Pallas kernels  186 us (97%)
  local copies, waits for them, and re-layouts  4.53 us (2%)
    pallas_call x1, Pallas kernels, per_device(): pl.pallas_call(kernel, out_shape=(jax.ShapeDtypeStruct((1024, 256), BF),...  186 us
    unnamed x7, local copies, waits for them, and re-layouts  4.53 us

profile of v1, /device:TPU:0, one launch (start us, length us, event | category | flops | bytes accessed | tf_op | source)
XLA Modules:
  0.0 190.9 jit_solution(1870298628021497429)
XLA Ops:
  0.6 185.7 %shard_map.76 = (bf16[1024,256]{1,0:T(8,128)(2,1)}, f32[512,512]{1,0:T(8,128)}, f32[512,512]{1,0:T(8,128)}) custom-call(bf16[1024,256]{1,0:T(8,128)(2,1)} %g_ref.1, bf16[1024,512]{1,0:T(8,128)(2,1)} %l_ref.1, bf16[512,256]{1,0:T(8,128)(2,1)} %r_ref.1, f32[512,512]{1,0:T(8,128)} %fm_ref.1, f32[512,512]{1,0:T(8,128)} %sm_ref.1), custom_call_target="tpu_custom_call" | custom-call | flops 12884901888 | bytes 6553600 | tf_op jit(solution)/shard_map/pallas_call | solution.py:436
  186.4 0.0 copy-start.1
  186.4 2.0 %copy.11 = bf16[1024,256]{1,0:T(8,128)(2,1)} copy(bf16[1024,256]{1,0:T(8,128)(2,1)} %get-tuple-element.6) | data formatting | bytes 1048576
  188.3 0.0 copy-done.1
  188.4 0.0 copy-start
  188.4 1.0 copy.12
  189.3 0.6 copy-done
  190.0 1.0 copy.13
Async XLA Ops:
  186.4 2.0 %copy-start.1 = (f32[512,512]{1,0:T(8,128)S(1)}, f32[512,512]{1,0:T(8,128)}, u32[]{:S(2)}) copy-start(f32[512,512]{1,0:T(8,128)} %get-tuple-element.7) | copy-start | bytes 3145732
  188.4 1.6 copy-start

commit v2 on v1

v2 whole, which is shorter than its diff:
```python
import functools

import jax
import jax.numpy as jnp
from jax import lax
from jax.experimental import pallas as pl
from jax.experimental.pallas import tpu as pltpu
from jax.sharding import PartitionSpec as P

MESH = pl.DeviceIdType.MESH
BF = jnp.bfloat16
F32 = jnp.float32
NK = 4
KC = 1024 // NK
NQ = 4
OPS = ("g", "trs", "tag", "rrs", "dag", "brs", "bag", "urs")


def wrap(v):
    return lax.rem(v + 8, 4)


def kernel(
    g_ref, l_ref, r_ref, fm_ref, sm_ref,
    u_ref, fn_ref, sn_ref,
    gx, rb, tp, tx, lh, pp, qq, rot_own, rot_home, d_home, dall, blp, blz, up, u_out, fm, sm,
    t_comb, t_fin, r_comb, r_fin, b_comb, b_fin, u_comb, u_fin,
    ring_s, ring_r, l_s, l_r, ra_s, ra_r, r1_s, r1_r, rsib_s, rsib_r, psib_s, psib_r,
    fwd_s, fwd_r, back_s, back_r, dsib_s, dsib_r, near,
):
    row, col = lax.axis_index("row"), lax.axis_index("col")
    y, c, x, z = row // 2, lax.rem(row, 2), col // 4, lax.rem(col, 4)
    other = 1 - c

    def dev(x, y, z, c):
        return (y * 2 + c, x * 4 + z)

    sib = dev(x, y, z, other)
    ring = {
        "x": (x, dev(wrap(x + 1), y, z, c), dev(wrap(x - 1), y, z, c)),
        "y": (y, dev(x, wrap(y + 1), z, c), dev(x, wrap(y - 1), z, c)),
        "z": (z, dev(x, y, wrap(z + 1), c), dev(x, y, wrap(z - 1), c)),
    }

    barrier = pltpu.get_barrier_semaphore()
    partners = [ring["x"][1], ring["x"][2], ring["y"][1], ring["y"][2], sib]
    for d in (1, 2, 3):
        partners += [dev(x, y, wrap(z + d), c), dev(x, y, wrap(z + d), other)]
    for partner in partners:
        pl.semaphore_signal(barrier, inc=1, device_id=partner, device_id_type=MESH)
    pl.semaphore_wait(barrier, len(partners))

    sent = []

    def send(src, dst, ssem, rsem, device):
        copy = pltpu.make_async_remote_copy(
            src_ref=src, dst_ref=dst, send_sem=ssem, recv_sem=rsem, device_id=device, device_id_type=MESH
        )
        copy.start()
        sent.append((None, copy))

    def local(src, dst, n):
        copy = pltpu.make_async_copy(src, dst, near.at[n])
        copy.start()
        return copy

    def arrived(dst, ssem, rsem):
        pltpu.make_async_remote_copy(
            src_ref=dst, dst_ref=dst, send_sem=ssem, recv_sem=rsem, device_id=sib, device_id_type=MESH
        ).wait_recv()

    def send_or_keep(mine, src, dst, ssem, rsem, device, by_copy=None):
        copy = pltpu.make_async_remote_copy(
            src_ref=src, dst_ref=dst, send_sem=ssem, recv_sem=rsem, device_id=device, device_id_type=MESH
        )

        @pl.when(jnp.logical_not(mine))
        def _():
            copy.start()

        @pl.when(mine)
        def _():
            if by_copy is None:
                dst[...] = src[...]
            else:
                kept = pltpu.make_async_copy(src, dst, by_copy)
                kept.start()
                kept.wait()

        sent.append((mine, copy))

    def arrived_or_kept(mine, dst, ssem, rsem):
        @pl.when(jnp.logical_not(mine))
        def _():
            arrived(dst, ssem, rsem)

    class Ring:
        def __init__(self, axis, ssem, rsem, half):
            self.pos, self.right_dev, self.left_dev = ring[axis]
            self.right, self.left, self.opp = wrap(self.pos + 1), wrap(self.pos - 1), wrap(self.pos + 2)
            self.ssem, self.rsem, self.half = ssem, rsem, half

        def go(self, j, n, src, dst):
            send(src, dst, self.ssem(j, n), self.rsem(j, n), self.right_dev if n < 3 else self.left_dev)

        def wait(self, j, n, dst):
            arrived(dst, self.ssem(j, n), self.rsem(j, n))

        def rows(self, j, h):
            if self.half is None:
                return (j // 2, pl.ds(2 * h, 2), j % 2)
            return (pl.ds((2 * j + h) * self.half, self.half),)

    class Gather(Ring):
        def __init__(self, axis, ssem, rsem, half, src, dst):
            super().__init__(axis, ssem, rsem, half)
            self.src, self.dst = src, dst

        def start(self, j):
            a, b = self.rows(j, 0), self.rows(j, 1)
            self.go(j, 0, self.src(a), self.dst(self.pos, a))
            self.go(j, 3, self.src(b), self.dst(self.pos, b))
            self.go(j, 1, self.src(b), self.dst(self.pos, b))
            self.go(j, 4, self.src(a), self.dst(self.pos, a))

        def mid(self, j):
            a, b = self.rows(j, 0), self.rows(j, 1)
            self.wait(j, 0, self.dst(self.left, a))
            self.go(j, 2, self.dst(self.left, a), self.dst(self.left, a))
            self.wait(j, 3, self.dst(self.right, b))
            self.go(j, 5, self.dst(self.right, b), self.dst(self.right, b))

        def end(self, j):
            a, b = self.rows(j, 0), self.rows(j, 1)
            self.wait(j, 1, self.dst(self.left, b))
            self.wait(j, 4, self.dst(self.right, a))
            self.wait(j, 2, self.dst(self.opp, a))
            self.wait(j, 5, self.dst(self.opp, b))

    class Scatter(Ring):
        def __init__(self, axis, ssem, rsem, half, piece, comb, fin, out):
            super().__init__(axis, ssem, rsem, half)
            self.piece, self.comb, self.fin, self.out = piece, comb, fin, out

        def start(self, j):
            a, b = self.rows(j, 0), self.rows(j, 1)
            self.go(j, 0, self.piece(self.opp, a), self.comb.at[j, 0])
            self.go(j, 3, self.piece(self.opp, b), self.comb.at[j, 1])
            self.go(j, 1, self.piece(self.right, b), self.fin.at[j, 0, 1])
            self.go(j, 4, self.piece(self.left, a), self.fin.at[j, 1, 0])

        def mid(self, j):
            a, b = self.rows(j, 0), self.rows(j, 1)
            for n, side, r, h in ((0, self.right, a, 0), (3, self.left, b, 1)):
                self.wait(j, n, self.comb.at[j, h])
                ref = self.piece(side, r)
                ref[...] = (ref[...].astype(F32) + self.comb[j, h].astype(F32)).astype(BF)
                self.go(j, n + 2, ref, self.fin.at[j, h, h])

        def end(self, j):
            for h, first, second in ((0, 4, 2), (1, 1, 5)):
                r = self.rows(j, h)
                self.wait(j, first, self.fin.at[j, 1 - h, h])
                self.wait(j, second, self.fin.at[j, h, h])
                total = self.piece(self.pos, r)[...].astype(F32)
                total = total + self.fin[j, 0, h].astype(F32) + self.fin[j, 1, h].astype(F32)
                self.out(r)[...] = total.astype(BF)

    def ring_sems(name):
        i = OPS.index(name)
        return (lambda j, n: ring_s.at[i, j, n]), (lambda j, n: ring_r.at[i, j, n])

    def columns(ref):
        return lambda t, r: ref.at[(*r, pl.ds(pl.multiple_of(t * 256, 256), 256))]

    def pieces(ref):
        return lambda t, r: ref.at[(t, *r)]

    kh = KC // 2
    g_ag = Gather("x", *ring_sems("g"), kh, lambda r: g_ref.at[r], columns(gx))
    t_rs = Scatter("z", *ring_sems("trs"), kh, pieces(tp), t_comb, t_fin, lambda r: tx.at[(x, *r)])
    t_ag = Gather("x", *ring_sems("tag"), kh, lambda r: tx.at[(x, *r)], pieces(tx))
    r_rs = Scatter("y", *ring_sems("rrs"), None, lambda t, r: pp.at[(c, t, *r)], r_comb, r_fin, lambda r: rot_own.at[r])
    d_ag = Gather("y", *ring_sems("dag"), None, lambda r: dall.at[(c, y, *r)], lambda t, r: dall.at[(c, t, *r)])
    b_rs = Scatter("x", *ring_sems("brs"), kh, pieces(blp), b_comb, b_fin, lambda r: columns(blz)(z, r))
    b_ag = Gather("z", *ring_sems("bag"), kh, lambda r: columns(blz)(z, r), columns(blz))
    u_rs = Scatter("x", *ring_sems("urs"), kh, pieces(up), u_comb, u_fin, lambda r: u_out.at[r])

    def l_unit(h, j):
        i = h * 2 + j

        def src(r):
            return l_ref.at[(*r, pl.ds(h * 256 + j * 128, 128))]

        def dst(t, r):
            return lh.at[(h, *r, pl.ds(pl.multiple_of(j * 512 + t * 128, 128), 128))]

        return Gather("z", lambda _, n: l_s.at[i, n], lambda _, n: l_r.at[i, n], 512, src, dst)

    l_units = [[l_unit(h, j) for h in range(2)] for j in range(2)]

    def rb_block(t, cc):
        return rb.at[pl.ds(pl.multiple_of(t * 256 + cc * 128, 128), 128)]

    def rb_rows(t, r):
        return rb.at[pl.ds(pl.multiple_of(t * 256 + c * 128 + r[0].start, 64), r[0].size)]

    r_ag = Gather("y", lambda _, n: ra_s.at[n], lambda _, n: ra_r.at[n], 64, lambda r: rb_rows(y, r), rb_rows)

    def rb_tile(cc, zz):
        return rb.at[
            pl.ds(pl.multiple_of(y * 256 + cc * 128, 128), 128), pl.ds(pl.multiple_of(zz * 256, 256), 256)
        ]

    for sl in range(2):
        for cc in range(2):
            mine = jnp.logical_and(2 * c + sl == z, c == cc)
            send_or_keep(
                mine, r_ref.at[pl.ds(sl * 256 + cc * 128, 128)], rb_tile(cc, z),
                r1_s.at[sl, cc], r1_r.at[z], dev(x, y, 2 * c + sl, cc), near.at[0],
            )
    g_ag.start(0)
    g_ag.start(1)
    for unit in l_units[0]:
        unit.start(0)
    own = [local(g_ref, gx.at[:, pl.ds(pl.multiple_of(x * 256, 256), 256)], 1)]
    for h in range(2):
        for j in range(2):
            own.append(local(
                l_ref.at[:, pl.ds(h * 256 + j * 128, 128)],
                lh.at[h, :, pl.ds(pl.multiple_of(j * 512 + z * 128, 128), 128)], 2 + h * 2 + j,
            ))
    moments = [local(fm_ref, fm, 6), local(sm_ref, sm, 7)]
    for zz in range(4):
        mine = jnp.logical_and(zz == z, z // 2 == c)
        arrived_or_kept(mine, rb_tile(c, zz), r1_s.at[0, 0], r1_r.at[zz])
    r_ag.start(0)

    def sib_block(t, n):
        send(rb_block(t, c), rb_block(t, c), rsib_s.at[n], rsib_r.at[n], sib)

    sib_block(y, 0)
    g_ag.mid(0)
    g_ag.start(2)
    g_ag.mid(1)
    g_ag.start(3)
    r_ag.mid(0)
    g_ag.mid(2)
    for unit in l_units[0]:
        unit.mid(0)
    g_ag.mid(3)
    r_ag.end(0)
    for n, t in enumerate((r_ag.left, r_ag.right, r_ag.opp)):
        sib_block(t, n + 1)
    for n, t in enumerate((y, r_ag.left, r_ag.right, r_ag.opp)):
        arrived(rb_block(t, other), rsib_s.at[n], rsib_r.at[n])

    def rotate_right(j):
        rows = pl.ds(j * KC, KC)

        def body(b, _):
            right = rb[:, pl.ds(pl.multiple_of(b * 256, 256), 256)]
            tp[b, rows] = jnp.dot(gx[rows], right, preferred_element_type=F32).astype(BF)
            return 0

        lax.fori_loop(0, 4, body, 0)

    for copy in own:
        copy.wait()

    def first(j):
        g_ag.end(j)
        rotate_right(j)
        t_rs.start(j)

    def second(j):
        t_rs.end(j)
        t_ag.start(j)

    first(0)
    first(1)
    t_rs.mid(0)
    first(2)
    t_rs.mid(1)
    first(3)
    t_rs.mid(2)
    second(0)
    t_rs.mid(3)
    for unit in l_units[1]:
        unit.start(0)
    second(1)
    t_ag.mid(0)
    second(2)
    t_ag.mid(1)
    second(3)
    t_ag.mid(2)
    t_ag.mid(3)
    for unit in l_units[1]:
        unit.mid(0)
    for j in range(NK):
        t_ag.end(j)

    def rotate_left(h, j):
        columns = pl.ds(j * 512, 512)

        def body(a, _):
            pp[h, a, j] = lax.dot_general(
                lh[h, :, columns], tx[a], (((0,), (0,)), ((), ())), preferred_element_type=F32
            ).astype(BF).reshape(4, 2, 64, 256)
            return 0

        lax.fori_loop(0, 4, body, 0)

    def rotate_left_both(j):
        for unit in l_units[j]:
            unit.end(0)
        rotate_left(other, j)
        for a in range(4):
            send(pp.at[other, a, j], qq.at[a, j], psib_s.at[j, a], psib_r.at[j, a], sib)
        rotate_left(c, j)

    def add_sibling(j):
        for a in range(4):
            arrived(qq.at[a, j], psib_s.at[j, a], psib_r.at[j, a])
            pp[c, a, j] = (pp[c, a, j].astype(F32) + qq[a, j].astype(F32)).astype(BF)
        r_rs.start(2 * j)
        r_rs.start(2 * j + 1)

    def home_rows(cc, q):
        return pl.ds(cc * 256 + q // 2 * 128 + q % 2 * 64, 64)

    def home_tile(ref, cc, s, q):
        return ref.at[
            pl.ds(pl.multiple_of(cc * 256 + q // 2 * 128 + q % 2 * 64, 64), 64),
            pl.ds(pl.multiple_of(s * 256, 256), 256),
        ]

    def to_home(q):
        r_rs.end(q)
        for d in range(4):
            zz = wrap(z + d)
            place = (rot_own.at[q // 2, zz, q % 2], home_tile(rot_home, c, lax.rem(z, 2), q),
                     fwd_s.at[q, d], fwd_r.at[q, lax.rem(z, 2) * 2 + c], dev(x, y, zz, z // 2))
            if d:
                send(*place)
            else:
                send_or_keep(z // 2 == c, *place)

    outs = []

    def moment_step(q):
        for s in range(2):
            for cc in range(2):
                mine = jnp.logical_and(2 * c + s == z, c == cc)
                arrived_or_kept(mine, home_tile(rot_home, cc, s, q), fwd_s.at[q, 0], fwd_r.at[q, s * 2 + cc])
        for h in range(2):
            rows = home_rows(h, q)
            rotated = rot_home[rows].astype(F32)
            first_new = 0.9 * fm[rows] + 0.1 * rotated
            second_new = 0.95 * sm[rows] + 0.05 * rotated * rotated
            fm[rows] = first_new
            sm[rows] = second_new
            d_home[rows] = (first_new / (jnp.sqrt(second_new) + 1e-08)).astype(BF)
        for h in range(2):
            for s in range(2):
                mine = jnp.logical_and(2 * c + s == z, c == h)
                send_or_keep(
                    mine, home_tile(d_home, h, s, q), dall.at[h, y, q // 2, z, q % 2],
                    back_s.at[q, h, s], back_r.at[q, z], dev(x, y, 2 * c + s, h),
                )

    def d_block(t, q, cc):
        return dall.at[cc, t, q // 2, :, q % 2]

    order = (y, d_ag.left, d_ag.right, d_ag.opp)

    def d_start(q):
        for zz in range(4):
            mine = jnp.logical_and(zz == z, z // 2 == c)
            arrived_or_kept(mine, dall.at[c, y, q // 2, zz, q % 2], back_s.at[q, 0, 0], back_r.at[q, zz])
        d_ag.start(q)
        send(d_block(y, q, c), d_block(y, q, c), dsib_s.at[q, 0], dsib_r.at[q, 0], sib)

    def d_end(q):
        d_ag.end(q)
        for n in (1, 2, 3):
            send(d_block(order[n], q, c), d_block(order[n], q, c), dsib_s.at[q, n], dsib_r.at[q, n], sib)

    def d_sibling(q):
        for n in range(4):
            arrived(d_block(order[n], q, other), dsib_s.at[q, n], dsib_r.at[q, n])

    rotate_left_both(0)
    add_sibling(0)
    r_rs.mid(0)
    rotate_left_both(1)
    r_rs.mid(1)
    for copy in moments:
        copy.wait()
    to_home(0)
    add_sibling(1)
    to_home(1)
    moment_step(0)
    r_rs.mid(2)
    moment_step(1)
    r_rs.mid(3)
    d_start(0)
    to_home(2)
    d_start(1)
    to_home(3)
    d_ag.mid(0)
    moment_step(2)
    d_ag.mid(1)
    moment_step(3)
    outs += [local(fm, fn_ref, 6), local(sm, sn_ref, 7)]
    d_start(2)
    d_end(0)
    d_start(3)
    d_end(1)
    d_ag.mid(2)
    d_ag.mid(3)
    d_end(2)
    d_end(3)
    for q in range(NQ):
        d_sibling(q)

    def rotate_back_left(j):
        rows = pl.ds(j * KC, KC)

        def body(a, _):
            total = jnp.dot(lh[0, rows], dall[0, a].reshape(1024, 256), preferred_element_type=F32)
            total = total + jnp.dot(lh[1, rows], dall[1, a].reshape(1024, 256), preferred_element_type=F32)
            blp[a, rows] = total.astype(BF)
            return 0

        lax.fori_loop(0, 4, body, 0)

    def rotate_back_right(j):
        rows = pl.ds(j * KC, KC)

        def body(t, _):
            right = rb[pl.ds(pl.multiple_of(t * 256, 256), 256)]
            up[t, rows] = lax.dot_general(
                blz[rows], right, (((1,), (1,)), ((), ())), preferred_element_type=F32
            ).astype(BF)
            return 0

        lax.fori_loop(0, 4, body, 0)

    def third(j):
        rotate_back_left(j)
        b_rs.start(j)

    def fourth(j):
        b_rs.end(j)
        b_ag.start(j)

    def fifth(j):
        b_ag.end(j)
        rotate_back_right(j)
        u_rs.start(j)

    def last(j):
        u_rs.end(j)
        rows = pl.ds(j * KC, KC)
        outs.append(local(u_out.at[rows], u_ref.at[rows], 8 + j))

    third(0)
    third(1)
    third(2)
    b_rs.mid(0)
    third(3)
    b_rs.mid(1)
    b_rs.mid(2)
    fourth(0)
    b_rs.mid(3)
    fourth(1)
    b_ag.mid(0)
    fourth(2)
    b_ag.mid(1)
    fourth(3)
    fifth(0)
    b_ag.mid(2)
    fifth(1)
    b_ag.mid(3)
    u_rs.mid(0)
    fifth(2)
    u_rs.mid(1)
    fifth(3)
    u_rs.mid(2)
    last(0)
    u_rs.mid(3)
    last(1)
    last(2)
    last(3)
    for copy in outs:
        copy.wait()
    for mine, copy in sent:
        if mine is None:
            copy.wait_send()
        else:
            @pl.when(jnp.logical_not(mine))
            def _(copy=copy):
                copy.wait_send()


def per_device(grad, basis_left, basis_right, first_moment, second_moment):
    dma = pltpu.SemaphoreType.DMA
    part = (2, 64, 256)
    m_rows = (2, 4, 2, 64, 256)

    def scatter_buffers(chunks, half):
        return [pltpu.VMEM((chunks, 2, *half), BF), pltpu.VMEM((chunks, 2, 2, *half), BF)]

    scratch = [
        pltpu.VMEM((1024, 1024), BF),
        pltpu.VMEM((1024, 1024), BF),
        pltpu.VMEM((4, 1024, 256), BF),
        pltpu.VMEM((4, 1024, 256), BF),
        pltpu.VMEM((2, 1024, 1024), BF),
        pltpu.VMEM((2, 4, *m_rows), BF),
        pltpu.VMEM((4, *m_rows), BF),
        pltpu.VMEM(m_rows, BF),
        pltpu.VMEM((512, 512), BF),
        pltpu.VMEM((512, 512), BF),
        pltpu.VMEM((2, 4, *m_rows), BF),
        pltpu.VMEM((4, 1024, 256), BF),
        pltpu.VMEM((1024, 1024), BF),
        pltpu.VMEM((4, 1024, 256), BF),
        pltpu.VMEM((1024, 256), BF),
        pltpu.VMEM((512, 512), F32),
        pltpu.VMEM((512, 512), F32),
    ]
    k_part = (KC // 2, 256)
    for chunks, half in ((NK, k_part), (NQ, part), (NK, k_part), (NK, k_part)):
        scratch += scatter_buffers(chunks, half)
    most = max(NK, NQ)
    for out, back in (
        ((len(OPS), most, 6), (len(OPS), most, 6)), ((4, 6), (4, 6)), ((6,), (6,)), ((2, 2), (4,)),
        ((4,), (4,)), ((2, 4), (2, 4)), ((NQ, 4), (NQ, 4)), ((NQ, 2, 2), (NQ, 4)), ((NQ, 4), (NQ, 4)),
    ):
        scratch += [dma(out), dma(back)]
    scratch.append(dma((8 + NK,)))
    anywhere = pl.BlockSpec(memory_space=pl.ANY)
    return pl.pallas_call(
        kernel,
        out_shape=(
            jax.ShapeDtypeStruct((1024, 256), BF),
            jax.ShapeDtypeStruct((512, 512), F32),
            jax.ShapeDtypeStruct((512, 512), F32),
        ),
        in_specs=[anywhere] * 5,
        out_specs=[anywhere] * 3,
        scratch_shapes=scratch,
        compiler_params=pltpu.CompilerParams(
            collective_id=0, has_side_effects=True, vmem_limit_bytes=60 * 1024 * 1024
        ),
        cost_estimate=pl.CostEstimate(flops=12884901888, bytes_accessed=6553600, transcendentals=262144),
    )(grad, basis_left, basis_right, first_moment, second_moment)


def solution(mesh):
    in_specs = (P("row", "col"), P("row", "col"), P("row", "col"), P("col", "row"), P("col", "row"))
    out_specs = (P("row", "col"), P("col", "row"), P("col", "row"))
    return jax.shard_map(
        per_device, mesh=mesh, in_specs=in_specs, out_specs=out_specs, check_vma=False
    )
```

time: 192 us -> 164 us (0.85)
  Pallas kernels: 186 us -> 159 us
    pallas_call x1, Pallas kernels: 186 us -> 159 us  [per_device(): pl.pallas_call(kernel, out_shape=(jax.ShapeDtypeStruct((1024, 256), BF),...]
where the time goes in v2:
time: 164 us
  Pallas kernels  159 us (97%)
  local copies, waits for them, and re-layouts  4.53 us (3%)
    pallas_call x1, Pallas kernels, per_device(): pl.pallas_call(kernel, out_shape=(jax.ShapeDtypeStruct((1024, 256), BF),...  159 us
    unnamed x7, local copies, waits for them, and re-layouts  4.53 us

profile of v2, /device:TPU:0, one launch (start us, length us, event | category | flops | bytes accessed | tf_op | source)
XLA Modules:
  0.0 164.1 jit_solution(15112092585166515132)
XLA Ops:
  0.6 158.9 %shard_map.76 = (bf16[1024,256]{1,0:T(8,128)(2,1)}, f32[512,512]{1,0:T(8,128)}, f32[512,512]{1,0:T(8,128)}) custom-call(bf16[1024,256]{1,0:T(8,128)(2,1)} %g_ref.1, bf16[1024,512]{1,0:T(8,128)(2,1)} %l_ref.1, bf16[512,256]{1,0:T(8,128)(2,1)} %r_ref.1, f32[512,512]{1,0:T(8,128)} %fm_ref.1, f32[512,512]{1,0:T(8,128)} %sm_ref.1), custom_call_target="tpu_custom_call" | custom-call | flops 12884901888 | bytes 6553600 | tf_op jit(solution)/shard_map/pallas_call | solution.py:545
  159.5 0.0 copy-start.1
  159.5 2.0 %copy.11 = bf16[1024,256]{1,0:T(8,128)(2,1)} copy(bf16[1024,256]{1,0:T(8,128)(2,1)} %get-tuple-element.6) | data formatting | bytes 1048576
  161.5 0.0 copy-done.1
  161.5 0.0 copy-start
  161.5 1.0 copy.12
  162.5 0.6 copy-done
  163.1 1.0 copy.13
Async XLA Ops:
  159.5 2.0 %copy-start.1 = (f32[512,512]{1,0:T(8,128)S(1)}, f32[512,512]{1,0:T(8,128)}, u32[]{:S(2)}) copy-start(f32[512,512]{1,0:T(8,128)} %get-tuple-element.7) | copy-start | bytes 3145732
  161.5 1.6 copy-start

commit v3 on v0

v3 whole, which is shorter than its diff:
```python
import functools

import jax
import jax.numpy as jnp
from jax import lax
from jax.experimental import pallas as pl
from jax.experimental.pallas import tpu as pltpu
from jax.sharding import PartitionSpec as P

MESH = pl.DeviceIdType.MESH
BF = jnp.bfloat16
F32 = jnp.float32
NJ = 4
NK = 4
KC = 1024 // NK
NG = 4


def wrap(v):
    return lax.rem(v + 8, 4)


def block(i, n):
    return pl.ds(pl.multiple_of(i * n, n), n)


def kernel(
    g_ref, l_ref, r_ref, fm_ref, sm_ref,
    u_ref, fn_ref, sn_ref,
    gz, lh, rr, lp, lq, lr, rp, rot, dx, ep, eq, ee, up, u_out, fm, sm,
    l_comb, l_fin, r_comb, r_fin, e_comb, e_fin, u_comb, u_fin,
    ring_s, ring_r, sib_r, turn_s, turn_r, cast_s, cast_r, near,
):
    row, col = lax.axis_index("row"), lax.axis_index("col")
    y, c, x, z = row // 2, lax.rem(row, 2), col // 4, lax.rem(col, 4)
    other = 1 - c

    def dev(x, y, z, c):
        return (y * 2 + c, x * 4 + z)

    sib = dev(x, y, z, other)
    ring = {
        "x": (x, dev(wrap(x + 1), y, z, c), dev(wrap(x - 1), y, z, c)),
        "y": (y, dev(x, wrap(y + 1), z, c), dev(x, wrap(y - 1), z, c)),
        "z": (z, dev(x, y, wrap(z + 1), c), dev(x, y, wrap(z - 1), c)),
    }

    barrier = pltpu.get_barrier_semaphore()
    partners = [*ring["x"][1:], *ring["y"][1:], *ring["z"][1:], dev(x, y, wrap(z + 2), c), sib]
    for partner in partners:
        pl.semaphore_signal(barrier, inc=1, device_id=partner, device_id_type=MESH)

    @pl.when(x != y)
    def _():
        for cc in range(2):
            pl.semaphore_signal(barrier, inc=1, device_id=dev(y, x, z, cc), device_id_type=MESH)

    pl.semaphore_wait(barrier, jnp.where(x != y, len(partners) + 2, len(partners)))

    def remote(src, dst, ssem, rsem, device):
        return pltpu.make_async_remote_copy(
            src_ref=src, dst_ref=dst, send_sem=ssem, recv_sem=rsem, device_id=device, device_id_type=MESH
        )

    def arrived(dst, rsem):
        remote(dst, dst, ring_s.at[0], rsem, sib).wait_recv()

    def local(src, dst, n):
        copy = pltpu.make_async_copy(src, dst, near.at[n])
        copy.start()
        return copy

    class Ring:
        count = 0
        sems = 0

        def __init__(self, axis, chunks, four):
            self.pos, self.right_dev, self.left_dev = ring[axis]
            self.right, self.left, self.opp = wrap(self.pos + 1), wrap(self.pos - 1), wrap(self.pos + 2)
            self.op, self.base, self.four = Ring.count, Ring.sems, four
            Ring.count += 1
            Ring.sems += 3 * chunks

        def rsem(self, j, n):
            return ring_r.at[self.base + 3 * j + {0: 0, 3: 1}.get(n, 2)]

        def go(self, j, n, src, dst):
            remote(src, dst, ring_s.at[self.op], self.rsem(j, n), self.right_dev if n < 3 else self.left_dev).start()

        def wait(self, j, n, dst):
            arrived(dst, self.rsem(j, n))

        def wait_four(self, j):
            arrived(self.four, self.rsem(j, 1))

    class Gather(Ring):
        def __init__(self, axis, chunks, four, src, dst):
            super().__init__(axis, chunks, four)
            self.src, self.dst = src, dst

        def start(self, j):
            self.go(j, 0, self.src(j, 0), self.dst(self.pos, j, 0))
            self.go(j, 3, self.src(j, 1), self.dst(self.pos, j, 1))
            self.go(j, 1, self.src(j, 1), self.dst(self.pos, j, 1))
            self.go(j, 4, self.src(j, 0), self.dst(self.pos, j, 0))

        def mid(self, j):
            self.wait(j, 0, self.dst(self.left, j, 0))
            self.go(j, 2, self.dst(self.left, j, 0), self.dst(self.left, j, 0))
            self.wait(j, 3, self.dst(self.right, j, 1))
            self.go(j, 5, self.dst(self.right, j, 1), self.dst(self.right, j, 1))

        def end(self, j):
            self.wait_four(j)

    class Scatter(Ring):
        def __init__(self, axis, chunks, four, piece, comb, fin, out):
            super().__init__(axis, chunks, four)
            self.piece, self.comb, self.fin, self.out = piece, comb, fin, out

        def start(self, j):
            self.go(j, 0, self.piece(self.opp, j, 0), self.comb.at[j, 0])
            self.go(j, 3, self.piece(self.opp, j, 1), self.comb.at[j, 1])
            self.go(j, 1, self.piece(self.right, j, 1), self.fin.at[j, 0, 1])
            self.go(j, 4, self.piece(self.left, j, 0), self.fin.at[j, 1, 0])

        def mid(self, j):
            for n, side, h in ((0, self.right, 0), (3, self.left, 1)):
                self.wait(j, n, self.comb.at[j, h])
                ref = self.piece(side, j, h)
                ref[...] = (ref[...].astype(F32) + self.comb[j, h].astype(F32)).astype(BF)
                self.go(j, n + 2, ref, self.fin.at[j, h, h])

        def end(self, j):
            self.wait_four(j)
            for h in range(2):
                total = self.piece(self.pos, j, h)[...].astype(F32)
                total = total + self.fin[j, 0, h].astype(F32) + self.fin[j, 1, h].astype(F32)
                self.out(j, h)[...] = total.astype(BF)

    def half_columns(ref):
        return lambda t, j, h: ref.at[j, pl.ds(2 * h, 2), c, :, block(t, 256)]

    def half_pieces(ref):
        return lambda t, j, h: ref.at[j, t, pl.ds(2 * h, 2), c]

    gh, kh = 1024 // NG // 2, KC // 2
    g_ag = Gather(
        "z", NG, lp.at[0, 0],
        lambda j, h: g_ref.at[pl.ds((2 * j + h) * gh, gh)],
        lambda t, j, h: gz.at[pl.ds((2 * j + h) * gh, gh), block(t, 256)],
    )
    l_ag = Gather(
        "x", NJ, lp.at[0, pl.ds(0, 2)],
        lambda j, h: l_ref.at[pl.ds(h * 512, 512), pl.ds(j * 128, 128)],
        lambda t, j, h: lh.at[j, pl.ds(h * 512, 512), block(t, 128)],
    )
    quarter = lp.at[0, 0]
    lr_rs = Scatter("y", NJ, quarter, half_pieces(lp), l_comb, l_fin, lambda j, h: half_columns(lr)(y, j, h))
    lr_ag = Gather("y", NJ, quarter, lambda j, h: half_columns(lr)(y, j, h), half_columns(lr))
    rot_rs = Scatter(
        "x", NJ, quarter, lambda t, j, h: rp.at[j, t, h], r_comb, r_fin,
        lambda j, h: rot.at[pl.ds(j * 128 + h * 64, 64)],
    )
    d_ag = Gather("x", NJ, quarter, lambda j, h: dx.at[j, x, h], lambda t, j, h: dx.at[j, t, h])
    e_rs = Scatter("y", NJ, quarter, half_pieces(ep), e_comb, e_fin, lambda j, h: half_columns(ee)(y, j, h))
    e_ag = Gather("y", NJ, quarter, lambda j, h: half_columns(ee)(y, j, h), half_columns(ee))
    u_rs = Scatter(
        "z", NK, quarter, lambda t, j, h: up.at[t, pl.ds(j * KC + h * kh, kh)], u_comb, u_fin,
        lambda j, h: u_out.at[pl.ds(j * KC + h * kh, kh)],
    )
    class Total:
        def __init__(self, rs, ag, parts, theirs, full, first):
            self.rs, self.ag, self.parts, self.theirs, self.full, self.first = rs, ag, parts, theirs, full, first
            self.ssem = ring_s.at[Ring.count + first // (2 * NJ)]

        def swap(self, j):
            remote(
                self.parts.at[j, :, :, other], self.theirs.at[j], self.ssem, sib_r.at[self.first + j], sib
            ).start()

        def add(self, j):
            arrived(self.theirs.at[j], sib_r.at[self.first + j])
            for t in range(4):
                mine = self.parts[j, t, :, c].astype(F32)
                self.parts[j, t, :, c] = (mine + self.theirs[j, t].astype(F32)).astype(BF)
            self.rs.start(j)

        def share(self, j, t):
            ref = self.full.at[j, :, c, :, block(t, 256)]
            remote(ref, ref, self.ssem, sib_r.at[self.first + NJ + j], sib).start()

        def turn(self, j):
            self.rs.end(j)
            self.ag.start(j)
            self.share(j, y)

        def end(self, j):
            self.ag.end(j)
            for t in (self.ag.left, self.ag.right, self.ag.opp):
                self.share(j, t)

        def ready(self, j):
            arrived(self.full.at[j, :, other], sib_r.at[self.first + NJ + j])

    lr_sum = Total(lr_rs, lr_ag, lp, lq, lr, 0)
    e_sum = Total(e_rs, e_ag, ep, eq, ee, 2 * NJ)

    root = z // 2 == c
    keep = jnp.logical_and(x == y, root)
    cols_here = block(lax.rem(z, 2), 256)
    turned = remote(r_ref, rr.at[block(c, 512), cols_here], turn_s.at[0], turn_r.at[c], dev(y, x, z, z // 2))
    casts = [
        remote(rr.at[:, cols_here], rr.at[:, cols_here], cast_s.at[d - 1], cast_r.at[lax.rem(z, 2)], dev(x, y, wrap(z + d), c))
        for d in (1, 2, 3)
    ]

    def right_send():
        @pl.when(jnp.logical_not(keep))
        def _():
            turned.start()

        @pl.when(keep)
        def _():
            pltpu.make_async_copy(r_ref, rr.at[block(c, 512), cols_here], near.at[0]).start()

    def right_cast():
        @pl.when(root)
        def _():
            for cc in range(2):
                here = jnp.logical_and(x == y, c == cc)

                @pl.when(here)
                def _():
                    pltpu.make_async_copy(r_ref, rr.at[pl.ds(cc * 512, 512), cols_here], near.at[0]).wait()

                @pl.when(jnp.logical_not(here))
                def _():
                    arrived(rr.at[pl.ds(cc * 512, 512), cols_here], turn_r.at[cc])

            for cast in casts:
                cast.start()

    def right_ready():
        for s in range(2):
            @pl.when(2 * c + s != z)
            def _():
                arrived(rr.at[:, pl.ds(s * 256, 256)], cast_r.at[s])

    def left_product(j):
        def body(t, _):
            lp[j, t] = lax.dot_general(
                lh[j], gz[:, block(t, 256)], (((0,), (0,)), ((), ())), preferred_element_type=F32
            ).astype(BF).reshape(4, 2, 64, 256)
            return 0

        lax.fori_loop(0, 4, body, 0)
        lr_sum.swap(j)

    def right_product(j):
        lr_sum.ready(j)
        rp[j] = jnp.dot(
            lr[j].reshape(512, 1024), rr[...], preferred_element_type=F32
        ).astype(BF).reshape(4, 2, 64, 512)
        rot_rs.start(j)

    outs = []

    def moment_step(j):
        rot_rs.end(j)
        for h in range(2):
            rows = pl.ds(j * 128 + h * 64, 64)
            rotated = rot[rows].astype(F32)
            first_new = 0.9 * fm[rows] + 0.1 * rotated
            second_new = 0.95 * sm[rows] + 0.05 * rotated * rotated
            fm[rows] = first_new
            sm[rows] = second_new
            dx[j, x, h] = (first_new / (jnp.sqrt(second_new) + 1e-08)).astype(BF)
        d_ag.start(j)

    def right_back(j):
        d_ag.end(j)

        def body(t, _):
            ep[j, t] = lax.dot_general(
                dx[j].reshape(512, 512), rr[block(t, 256)], (((1,), (1,)), ((), ())), preferred_element_type=F32
            ).astype(BF).reshape(4, 2, 64, 256)
            return 0

        lax.fori_loop(0, 4, body, 0)
        e_sum.swap(j)

    def left_back(k):
        rows = pl.ds(k * KC, KC)

        def body(t, _):
            total = jnp.zeros((KC, 256), F32)
            for j in range(NJ):
                right = ee[j, :, :, :, block(t, 256)].reshape(512, 256)
                total = total + jnp.dot(lh[j, rows], right, preferred_element_type=F32)
            up[t, rows] = total.astype(BF)
            return 0

        lax.fori_loop(0, 4, body, 0)
        u_rs.start(k)

    def last(k):
        u_rs.end(k)
        rows = pl.ds(k * KC, KC)
        outs.append(local(u_out.at[rows], u_ref.at[rows], 4 + k))

    l_ag.start(0)
    l_ag.start(1)
    g_ag.start(0)
    own = [local(g_ref, gz.at[:, block(z, 256)], 1)]
    for j in range(4):
        own.append(local(l_ref.at[:, pl.ds(j * 128, 128)], lh.at[j, :, block(x, 128)], 4 + j))
    moments = [local(fm_ref, fm, 2), local(sm_ref, sm, 3)]
    g_ag.mid(0)
    g_ag.start(1)
    g_ag.start(2)
    g_ag.start(3)
    l_ag.mid(0)
    g_ag.mid(1)
    l_ag.mid(1)
    g_ag.mid(2)
    right_send()
    l_ag.start(2)
    l_ag.start(3)
    g_ag.mid(3)
    for copy in own:
        copy.wait()
    l_ag.end(1)
    g_ag.end(0)
    g_ag.end(1)
    g_ag.end(2)
    g_ag.end(3)
    left_product(1)
    lr_sum.add(1)
    l_ag.end(0)
    left_product(0)
    right_cast()
    lr_rs.mid(1)
    lr_sum.add(0)
    lr_sum.turn(1)
    lr_rs.mid(0)
    l_ag.mid(3)
    l_ag.mid(2)
    lr_ag.mid(1)
    lr_sum.turn(0)
    lr_sum.end(1)
    l_ag.end(3)
    left_product(3)
    right_ready()
    right_product(1)
    lr_ag.mid(0)
    l_ag.end(2)
    left_product(2)
    lr_sum.add(3)
    rot_rs.mid(1)
    lr_sum.end(0)
    right_product(0)
    lr_rs.mid(3)
    lr_sum.add(2)
    for copy in moments:
        copy.wait()
    moment_step(1)
    rot_rs.mid(0)
    lr_sum.turn(3)
    lr_rs.mid(2)
    d_ag.mid(1)
    lr_ag.mid(3)
    moment_step(0)
    lr_sum.turn(2)
    right_back(1)
    lr_sum.end(3)
    d_ag.mid(0)
    lr_ag.mid(2)
    e_sum.add(1)
    right_product(3)
    lr_sum.end(2)
    right_back(0)
    rot_rs.mid(3)
    right_product(2)
    e_sum.add(0)
    moment_step(3)
    rot_rs.mid(2)
    e_rs.mid(1)
    e_rs.mid(0)
    d_ag.mid(3)
    e_sum.turn(1)
    moment_step(2)
    outs += [local(fm, fn_ref, 2), local(sm, sn_ref, 3)]
    e_sum.turn(0)
    right_back(3)
    e_ag.mid(1)
    d_ag.mid(2)
    e_sum.add(3)
    e_ag.mid(0)
    right_back(2)
    e_rs.mid(3)
    e_sum.add(2)
    e_sum.end(0)
    e_rs.mid(2)
    e_sum.turn(3)
    e_sum.end(1)
    e_sum.turn(2)
    e_ag.mid(3)
    e_ag.mid(2)
    e_sum.end(3)
    e_sum.end(2)
    for j in range(NJ):
        e_sum.ready(j)
    left_back(1)
    left_back(3)
    left_back(0)
    u_rs.mid(1)
    left_back(2)
    u_rs.mid(3)
    u_rs.mid(0)
    last(1)
    u_rs.mid(2)
    last(3)
    last(0)
    last(2)
    for copy in outs:
        copy.wait()

    for op in range(Ring.count):
        whole = lp.at[pl.ds(0, 3)] if op == l_ag.op else lp.at[pl.ds(0, 3), pl.ds(0, 2)]
        remote(whole, whole, ring_s.at[op], ring_r.at[0], sib).wait_send()
    for total in (lr_sum, e_sum):
        remote(lh, lh, total.ssem, ring_r.at[0], sib).wait_send()

    @pl.when(jnp.logical_not(keep))
    def _():
        turned.wait_send()

    @pl.when(root)
    def _():
        for cast in casts:
            cast.wait_send()


def per_device(grad, basis_left, basis_right, first_moment, second_moment):
    dma = pltpu.SemaphoreType.DMA

    def scatter_buffers(chunks, half):
        return [pltpu.VMEM((chunks, 2, *half), BF), pltpu.VMEM((chunks, 2, 2, *half), BF)]

    scratch = [
        pltpu.VMEM((1024, 1024), BF),
        pltpu.VMEM((NJ, 1024, 512), BF),
        pltpu.VMEM((1024, 512), BF),
        pltpu.VMEM((NJ, 4, 4, 2, 64, 256), BF),
        pltpu.VMEM((NJ, 4, 4, 64, 256), BF),
        pltpu.VMEM((NJ, 4, 2, 64, 1024), BF),
        pltpu.VMEM((NJ, 4, 2, 64, 512), BF),
        pltpu.VMEM((512, 512), BF),
        pltpu.VMEM((NJ, 4, 2, 64, 512), BF),
        pltpu.VMEM((NJ, 4, 4, 2, 64, 256), BF),
        pltpu.VMEM((NJ, 4, 4, 64, 256), BF),
        pltpu.VMEM((NJ, 4, 2, 64, 1024), BF),
        pltpu.VMEM((4, 1024, 256), BF),
        pltpu.VMEM((1024, 256), BF),
        pltpu.VMEM((512, 512), F32),
        pltpu.VMEM((512, 512), F32),
    ]
    for chunks, half in ((NJ, (2, 64, 256)), (NJ, (64, 512)), (NJ, (2, 64, 256)), (NK, (KC // 2, 256))):
        scratch += scatter_buffers(chunks, half)
    scratch += [dma((n,)) for n in (11, 3 * (NG + 7 * NJ + NK), 4 * NJ, 1, 2, 3, 2, 8)]
    anywhere = pl.BlockSpec(memory_space=pl.ANY)
    return pl.pallas_call(
        kernel,
        out_shape=(
            jax.ShapeDtypeStruct((1024, 256), BF),
            jax.ShapeDtypeStruct((512, 512), F32),
            jax.ShapeDtypeStruct((512, 512), F32),
        ),
        in_specs=[anywhere] * 5,
        out_specs=[anywhere] * 3,
        scratch_shapes=scratch,
        compiler_params=pltpu.CompilerParams(
            collective_id=0, has_side_effects=True, vmem_limit_bytes=60 * 1024 * 1024
        ),
        cost_estimate=pl.CostEstimate(flops=12884901888, bytes_accessed=6553600, transcendentals=262144),
    )(grad, basis_left, basis_right, first_moment, second_moment)


def solution(mesh):
    in_specs = (P("row", "col"), P("row", "col"), P("row", "col"), P("col", "row"), P("col", "row"))
    out_specs = (P("row", "col"), P("col", "row"), P("col", "row"))
    return jax.shard_map(
        per_device, mesh=mesh, in_specs=in_specs, out_specs=out_specs, check_vma=False
    )
```

time: 482 us -> 152 us (0.32)
  waiting for transfers between devices: 432 us -> 0 us
  Pallas kernels: 0 us -> 145 us
  matrix products: 32.6 us -> 0 us
  between operations: 14.1 us -> 0.65 us
    reduce_scatter x4 -> x0, waiting for transfers between devices: 250 us -> none  [the longest x2 173 us: rotate_backward(): lax.psum_scatter(partial_terms.astype(jnp.bfloat16), 'col', scatter_dimen...]
    all_gather x4 -> x0, waiting for transfers between devices: 180 us -> none  [the longest x2 132 us: rotate_forward(): lax.all_gather(moving_matrix, 'col', axis=1, tiled=True)]
    pallas_call x0 -> x1, Pallas kernels: none -> 145 us  [per_device(): pl.pallas_call(kernel, out_shape=(jax.ShapeDtypeStruct((1024, 256), BF),...]
    dot_general x4 -> x0, matrix products: 32.6 us -> none  [the longest x2 16.5 us: product(): lax.dot_general(left_matrix, pieces, (((1,), (1,)), ((), ())), preferred_...]
  transfers between devices with their start and end apart: 8 -> 0, of which waited for: 8 -> 0; matrix products, arithmetic and copies ran while one was open for 4% -> 0% of each run, Pallas kernels for 0% -> 0%
where the time goes in v3:
time: 152 us; the launch traced here: 150 us
  Pallas kernels  145 us (95%)
  local copies, waits for them, and re-layouts  4.53 us (3%)
    pallas_call x1, Pallas kernels, per_device(): pl.pallas_call(kernel, out_shape=(jax.ShapeDtypeStruct((1024, 256), BF),...  145 us
    unnamed x7, local copies, waits for them, and re-layouts  4.53 us

profile of v3, /device:TPU:0, one launch (start us, length us, event | category | flops | bytes accessed | tf_op | source)
XLA Modules:
  0.0 150.5 jit_solution(302325632352750999)
XLA Ops:
  0.6 145.3 %shard_map.76 = (bf16[1024,256]{1,0:T(8,128)(2,1)}, f32[512,512]{1,0:T(8,128)}, f32[512,512]{1,0:T(8,128)}) custom-call(bf16[1024,256]{1,0:T(8,128)(2,1)} %g_ref.1, bf16[1024,512]{1,0:T(8,128)(2,1)} %l_ref.1, bf16[512,256]{1,0:T(8,128)(2,1)} %r_ref.1, f32[512,512]{1,0:T(8,128)} %fm_ref.1, f32[512,512]{1,0:T(8,128)} %sm_ref.1), custom_call_target="tpu_custom_call" | custom-call | flops 12884901888 | bytes 6553600 | tf_op jit(solution)/shard_map/pallas_call | solution.py:473
  145.9 0.0 copy-start.1
  145.9 2.0 %copy.11 = bf16[1024,256]{1,0:T(8,128)(2,1)} copy(bf16[1024,256]{1,0:T(8,128)(2,1)} %get-tuple-element.6) | data formatting | bytes 1048576
  147.9 0.0 copy-done.1
  147.9 0.0 copy-start
  147.9 1.0 copy.12
  148.9 0.6 copy-done
  149.5 1.0 copy.13
Async XLA Ops:
  145.9 2.0 %copy-start.1 = (f32[512,512]{1,0:T(8,128)S(1)}, f32[512,512]{1,0:T(8,128)}, u32[]{:S(2)}) copy-start(f32[512,512]{1,0:T(8,128)} %get-tuple-element.7) | copy-start | bytes 3145732
  147.9 1.6 %copy-start = (f32[512,512]{1,0:T(8,128)S(1)}, f32[512,512]{1,0:T(8,128)}, u32[]{:S(2)}) copy-start(f32[512,512]{1,0:T(8,128)} %get-tuple-element.8) | copy-start | bytes 3145732

commit v4 on v3

--- a/solution.py
+++ b/solution.py
@@ -248,13 +248,9 @@
                 arrived(rr.at[:, pl.ds(s * 256, 256)], cast_r.at[s])
 
     def left_product(j):
-        def body(t, _):
-            lp[j, t] = lax.dot_general(
-                lh[j], gz[:, block(t, 256)], (((0,), (0,)), ((), ())), preferred_element_type=F32
-            ).astype(BF).reshape(4, 2, 64, 256)
-            return 0
-
-        lax.fori_loop(0, 4, body, 0)
+        part = lax.dot_general(lh[j], gz[...], (((0,), (0,)), ((), ())), preferred_element_type=F32).astype(BF)
+        for t in range(4):
+            lp[j, t] = part[:, t * 256 : t * 256 + 256].reshape(4, 2, 64, 256)
         lr_sum.swap(j)
 
     def right_product(j):
@@ -281,27 +277,21 @@
     def right_back(j):
         d_ag.end(j)
 
-        def body(t, _):
-            ep[j, t] = lax.dot_general(
-                dx[j].reshape(512, 512), rr[block(t, 256)], (((1,), (1,)), ((), ())), preferred_element_type=F32
-            ).astype(BF).reshape(4, 2, 64, 256)
-            return 0
-
-        lax.fori_loop(0, 4, body, 0)
+        part = lax.dot_general(
+            dx[j].reshape(512, 512), rr[...], (((1,), (1,)), ((), ())), preferred_element_type=F32
+        ).astype(BF)
+        for t in range(4):
+            ep[j, t] = part[:, t * 256 : t * 256 + 256].reshape(4, 2, 64, 256)
         e_sum.swap(j)
 
     def left_back(k):
         rows = pl.ds(k * KC, KC)
 
-        def body(t, _):
-            total = jnp.zeros((KC, 256), F32)
-            for j in range(NJ):
-                right = ee[j, :, :, :, block(t, 256)].reshape(512, 256)
-                total = total + jnp.dot(lh[j, rows], right, preferred_element_type=F32)
-            up[t, rows] = total.astype(BF)
-            return 0
-
-        lax.fori_loop(0, 4, body, 0)
+        total = jnp.dot(lh[0, rows], ee[0].reshape(512, 1024), preferred_element_type=F32)
+        for j in range(1, NJ):
+            total = total + jnp.dot(lh[j, rows], ee[j].reshape(512, 1024), preferred_element_type=F32)
+        for t in range(4):
+            up[t, rows] = total[:, t * 256 : t * 256 + 256].astype(BF)
         u_rs.start(k)
 
     def last(k):
@@ -470,7 +460,7 @@
         scratch += scatter_buffers(chunks, half)
     scratch += [dma((n,)) for n in (11, 3 * (NG + 7 * NJ + NK), 4 * NJ, 1, 2, 3, 2, 8)]
     anywhere = pl.BlockSpec(memory_space=pl.ANY)
-    return pl.pallas_call(
+    results = pl.pallas_call(
         kernel,
         out_shape=(
             jax.ShapeDtypeStruct((1024, 256), BF),
@@ -486,6 +476,32 @@
         cost_estimate=pl.CostEstimate(flops=12884901888, bytes_accessed=6553600, transcendentals=262144),
     )(grad, basis_left, basis_right, first_moment, second_moment)
 
+    def hand_over(u, fn, sn, u_out, fn_out, sn_out, u_held, fn_held, sn_held, sems):
+        steps = []
+        for i, (src, held, dst) in enumerate(((u, u_held, u_out), (fn, fn_held, fn_out), (sn, sn_held, sn_out))):
+            rows = src.shape[0] // 2
+            for part in range(2):
+                here, sem = pl.ds(part * rows, rows), sems.at[2 * i + part]
+                steps.append((
+                    pltpu.make_async_copy(src.at[here], held.at[here], sem),
+                    pltpu.make_async_copy(held.at[here], dst.at[here], sem),
+                ))
+                steps[-1][0].start()
+        for come, leave in steps:
+            come.wait()
+            leave.start()
+        for _, leave in steps:
+            leave.wait()
+
+    return pl.pallas_call(
+        hand_over,
+        out_shape=tuple(jax.ShapeDtypeStruct(r.shape, r.dtype) for r in results),
+        in_specs=[anywhere] * 3,
+        out_specs=[anywhere] * 3,
+        scratch_shapes=[*(pltpu.VMEM(r.shape, r.dtype) for r in results), dma((6,))],
+        cost_estimate=pl.CostEstimate(flops=0, bytes_accessed=5242880, transcendentals=0),
+    )(*results)
+
 
 def solution(mesh):
     in_specs = (P("row", "col"), P("row", "col"), P("row", "col"), P("col", "row"), P("col", "row"))

time: 152 us -> 146 us (0.961)
  local copies, waits for them, and re-layouts: 4.53 us -> 0 us
    unnamed x7 -> x0, local copies, waits for them, and re-layouts: 4.53 us -> none
    pallas_call x1, Pallas kernels: 145 us -> 141 us  [per_device(): pl.pallas_call(kernel, out_shape=(jax.ShapeDtypeStruct((1024, 256), BF),...]
    pallas_call x0 -> x1, Pallas kernels: none -> 2.56 us  [per_device(): pl.pallas_call(hand_over, out_shape=tuple((jax.ShapeDtypeStruct(r.shape,...]
where the time goes in v4:
time: 146 us; the launch traced here: 145 us
  Pallas kernels  144 us (99%)
    pallas_call x1, Pallas kernels, per_device(): pl.pallas_call(kernel, out_shape=(jax.ShapeDtypeStruct((1024, 256), BF),...  141 us

profile of v4, /device:TPU:0, one launch (start us, length us, event | category | flops | bytes accessed | tf_op | source)
XLA Modules:
  0.0 144.6 jit_solution(11319747321738356131)
XLA Ops:
  0.6 141.2 %shard_map.76 = (bf16[1024,256]{1,0:T(8,128)(2,1)}, f32[512,512]{1,0:T(8,128)}, f32[512,512]{1,0:T(8,128)}) custom-call(bf16[1024,256]{1,0:T(8,128)(2,1)} %g_ref.1, bf16[1024,512]{1,0:T(8,128)(2,1)} %l_ref.1, bf16[512,256]{1,0:T(8,128)(2,1)} %r_ref.1, f32[512,512]{1,0:T(8,128)} %fm_ref.1, f32[512,512]{1,0:T(8,128)} %sm_ref.1), custom_call_target="tpu_custom_call" | custom-call | flops 12884901888 | bytes 6553600 | tf_op jit(solution)/shard_map/pallas_call | solution.py:463
  141.9 2.6 %shard_map.77 = (bf16[1024,256]{1,0:T(8,128)(2,1)}, f32[512,512]{1,0:T(8,128)}, f32[512,512]{1,0:T(8,128)}) custom-call(bf16[1024,256]{1,0:T(8,128)(2,1)} %get-tuple-element.6.u, f32[512,512]{1,0:T(8,128)} %get-tuple-element.7.fn, f32[512,512]{1,0:T(8,128)} %get-tuple-element.8.sn), custom_call_target="tpu_custom_call" | custom-call | bytes 5242880 | tf_op jit(solution)/shard_map/pallas_call | solution.py:496

commit v5 on v4

--- a/solution.py
+++ b/solution.py
@@ -11,7 +11,8 @@
 BF = jnp.bfloat16
 F32 = jnp.float32
 NJ = 4
-NK = 4
+NK = 2
+NP = 2
 KC = 1024 // NK
 NG = 4
 
@@ -74,28 +75,28 @@
         count = 0
         sems = 0
 
-        def __init__(self, axis, chunks, four):
+        def __init__(self, axis, chunks, two, four):
             self.pos, self.right_dev, self.left_dev = ring[axis]
             self.right, self.left, self.opp = wrap(self.pos + 1), wrap(self.pos - 1), wrap(self.pos + 2)
-            self.op, self.base, self.four = Ring.count, Ring.sems, four
+            self.op, self.base, self.two, self.four = Ring.count, Ring.sems, two, four
             Ring.count += 1
-            Ring.sems += 3 * chunks
+            Ring.sems += 2 * chunks
 
         def rsem(self, j, n):
-            return ring_r.at[self.base + 3 * j + {0: 0, 3: 1}.get(n, 2)]
+            return ring_r.at[self.base + 2 * j + (n not in (0, 3))]
 
         def go(self, j, n, src, dst):
             remote(src, dst, ring_s.at[self.op], self.rsem(j, n), self.right_dev if n < 3 else self.left_dev).start()
 
-        def wait(self, j, n, dst):
-            arrived(dst, self.rsem(j, n))
+        def wait_two(self, j):
+            arrived(self.two, self.rsem(j, 0))
 
         def wait_four(self, j):
             arrived(self.four, self.rsem(j, 1))
 
     class Gather(Ring):
-        def __init__(self, axis, chunks, four, src, dst):
-            super().__init__(axis, chunks, four)
+        def __init__(self, axis, chunks, two, four, src, dst):
+            super().__init__(axis, chunks, two, four)
             self.src, self.dst = src, dst
 
         def start(self, j):
@@ -105,17 +106,16 @@
             self.go(j, 4, self.src(j, 0), self.dst(self.pos, j, 0))
 
         def mid(self, j):
-            self.wait(j, 0, self.dst(self.left, j, 0))
+            self.wait_two(j)
             self.go(j, 2, self.dst(self.left, j, 0), self.dst(self.left, j, 0))
-            self.wait(j, 3, self.dst(self.right, j, 1))
             self.go(j, 5, self.dst(self.right, j, 1), self.dst(self.right, j, 1))
 
         def end(self, j):
             self.wait_four(j)
 
     class Scatter(Ring):
-        def __init__(self, axis, chunks, four, piece, comb, fin, out):
-            super().__init__(axis, chunks, four)
+        def __init__(self, axis, chunks, two, four, piece, comb, fin, out):
+            super().__init__(axis, chunks, two, four)
             self.piece, self.comb, self.fin, self.out = piece, comb, fin, out
 
         def start(self, j):
@@ -125,8 +125,8 @@
             self.go(j, 4, self.piece(self.left, j, 0), self.fin.at[j, 1, 0])
 
         def mid(self, j):
+            self.wait_two(j)
             for n, side, h in ((0, self.right, 0), (3, self.left, 1)):
-                self.wait(j, n, self.comb.at[j, h])
                 ref = self.piece(side, j, h)
                 ref[...] = (ref[...].astype(F32) + self.comb[j, h].astype(F32)).astype(BF)
                 self.go(j, n + 2, ref, self.fin.at[j, h, h])
@@ -138,41 +138,46 @@
                 total = total + self.fin[j, 0, h].astype(F32) + self.fin[j, 1, h].astype(F32)
                 self.out(j, h)[...] = total.astype(BF)
 
-    def half_columns(ref):
-        return lambda t, j, h: ref.at[j, pl.ds(2 * h, 2), c, :, block(t, 256)]
+    def half_columns(ref, width=256):
+        return lambda t, j, h: ref.at[j, pl.ds(2 * h, 2), c, :, block(t, width)]
 
     def half_pieces(ref):
         return lambda t, j, h: ref.at[j, t, pl.ds(2 * h, 2), c]
 
+    small = lp.at[0, 0, 0], lp.at[0, 0, pl.ds(0, 2)]
+    middle = lp.at[0, 0, pl.ds(0, 2)], lp.at[0, 0]
+    large = lp.at[0, 0], lp.at[0, pl.ds(0, 2)]
     gh, kh = 1024 // NG // 2, KC // 2
     g_ag = Gather(
-        "z", NG, lp.at[0, 0],
+        "z", NG, *middle,
         lambda j, h: g_ref.at[pl.ds((2 * j + h) * gh, gh)],
         lambda t, j, h: gz.at[pl.ds((2 * j + h) * gh, gh), block(t, 256)],
     )
     l_ag = Gather(
-        "x", NJ, lp.at[0, pl.ds(0, 2)],
+        "x", NJ, *large,
         lambda j, h: l_ref.at[pl.ds(h * 512, 512), pl.ds(j * 128, 128)],
         lambda t, j, h: lh.at[j, pl.ds(h * 512, 512), block(t, 128)],
     )
-    quarter = lp.at[0, 0]
-    lr_rs = Scatter("y", NJ, quarter, half_pieces(lp), l_comb, l_fin, lambda j, h: half_columns(lr)(y, j, h))
-    lr_ag = Gather("y", NJ, quarter, lambda j, h: half_columns(lr)(y, j, h), half_columns(lr))
+    lr_rs = Scatter("y", NJ, *middle, half_pieces(lp), l_comb, l_fin, lambda j, h: half_columns(lr)(y, j, h))
+    lr_ag = Gather("y", NJ, *middle, lambda j, h: half_columns(lr)(y, j, h), half_columns(lr))
     rot_rs = Scatter(
-        "x", NJ, quarter, lambda t, j, h: rp.at[j, t, h], r_comb, r_fin,
+        "x", NJ, *middle, lambda t, j, h: rp.at[j, t, h], r_comb, r_fin,
         lambda j, h: rot.at[pl.ds(j * 128 + h * 64, 64)],
     )
-    d_ag = Gather("x", NJ, quarter, lambda j, h: dx.at[j, x, h], lambda t, j, h: dx.at[j, t, h])
-    e_rs = Scatter("y", NJ, quarter, half_pieces(ep), e_comb, e_fin, lambda j, h: half_columns(ee)(y, j, h))
-    e_ag = Gather("y", NJ, quarter, lambda j, h: half_columns(ee)(y, j, h), half_columns(ee))
+    d_ag = Gather("x", NJ, *middle, lambda j, h: dx.at[j, x, h], lambda t, j, h: dx.at[j, t, h])
+    e_half = half_columns(ee, 128)
+    e_rs = Scatter("y", NP * NJ, *small, half_pieces(ep), e_comb, e_fin, lambda j, h: e_half(y, j, h))
+    e_ag = Gather("y", NP * NJ, *small, lambda j, h: e_half(y, j, h), e_half)
     u_rs = Scatter(
-        "z", NK, quarter, lambda t, j, h: up.at[t, pl.ds(j * KC + h * kh, kh)], u_comb, u_fin,
-        lambda j, h: u_out.at[pl.ds(j * KC + h * kh, kh)],
+        "z", NP * NK, *middle, lambda t, j, h: up.at[j // NK, t, pl.ds(j % NK * KC + h * kh, kh)], u_comb, u_fin,
+        lambda j, h: u_out.at[pl.ds(j % NK * KC + h * kh, kh), pl.ds(j // NK * 128, 128)],
     )
+
     class Total:
-        def __init__(self, rs, ag, parts, theirs, full, first):
-            self.rs, self.ag, self.parts, self.theirs, self.full, self.first = rs, ag, parts, theirs, full, first
-            self.ssem = ring_s.at[Ring.count + first // (2 * NJ)]
+        def __init__(self, rs, ag, parts, theirs, full, width, first, count):
+            self.rs, self.ag, self.parts, self.theirs, self.full = rs, ag, parts, theirs, full
+            self.width, self.first, self.count = width, first, count
+            self.ssem = ring_s.at[Ring.count + (first > 0)]
 
         def swap(self, j):
             remote(
@@ -187,8 +192,8 @@
             self.rs.start(j)
 
         def share(self, j, t):
-            ref = self.full.at[j, :, c, :, block(t, 256)]
-            remote(ref, ref, self.ssem, sib_r.at[self.first + NJ + j], sib).start()
+            ref = self.full.at[j, :, c, :, block(t, self.width)]
+            remote(ref, ref, self.ssem, sib_r.at[self.first + self.count + j], sib).start()
 
         def turn(self, j):
             self.rs.end(j)
@@ -201,17 +206,17 @@
                 self.share(j, t)
 
         def ready(self, j):
-            arrived(self.full.at[j, :, other], sib_r.at[self.first + NJ + j])
-
-    lr_sum = Total(lr_rs, lr_ag, lp, lq, lr, 0)
-    e_sum = Total(e_rs, e_ag, ep, eq, ee, 2 * NJ)
+            arrived(self.full.at[j, :, other], sib_r.at[self.first + self.count + j])
+
+    lr_sum = Total(lr_rs, lr_ag, lp, lq, lr, 256, 0, NJ)
+    e_sum = Total(e_rs, e_ag, ep, eq, ee, 128, 2 * NJ, NP * NJ)
 
     root = z // 2 == c
     keep = jnp.logical_and(x == y, root)
     cols_here = block(lax.rem(z, 2), 256)
-    turned = remote(r_ref, rr.at[block(c, 512), cols_here], turn_s.at[0], turn_r.at[c], dev(y, x, z, z // 2))
+    turned = remote(r_ref, rr.at[pl.ds(2 * c, 2), :, :, cols_here], turn_s.at[0], turn_r.at[c], dev(y, x, z, z // 2))
     casts = [
-        remote(rr.at[:, cols_here], rr.at[:, cols_here], cast_s.at[d - 1], cast_r.at[lax.rem(z, 2)], dev(x, y, wrap(z + d), c))
+        remote(rr.at[:, :, :, cols_here], rr.at[:, :, :, cols_here], cast_s.at[d - 1], cast_r.at[lax.rem(z, 2)], dev(x, y, wrap(z + d), c))
         for d in (1, 2, 3)
     ]
 
@@ -222,7 +227,7 @@
 
         @pl.when(keep)
         def _():
-            pltpu.make_async_copy(r_ref, rr.at[block(c, 512), cols_here], near.at[0]).start()
+            pltpu.make_async_copy(r_ref, rr.at[pl.ds(2 * c, 2), :, :, cols_here], near.at[0]).start()
 
     def right_cast():
         @pl.when(root)
@@ -232,11 +237,11 @@
 
                 @pl.when(here)
                 def _():
-                    pltpu.make_async_copy(r_ref, rr.at[pl.ds(cc * 512, 512), cols_here], near.at[0]).wait()
+                    pltpu.make_async_copy(r_ref, rr.at[pl.ds(cc * 2, 2), :, :, cols_here], near.at[0]).wait()
 
                 @pl.when(jnp.logical_not(here))
                 def _():
-                    arrived(rr.at[pl.ds(cc * 512, 512), cols_here], turn_r.at[cc])
+                    arrived(rr.at[pl.ds(cc * 2, 2), :, :, cols_here], turn_r.at[cc])
 
             for cast in casts:
                 cast.start()
@@ -245,7 +250,7 @@
         for s in range(2):
             @pl.when(2 * c + s != z)
             def _():
-                arrived(rr.at[:, pl.ds(s * 256, 256)], cast_r.at[s])
+                arrived(rr.at[:, :, :, pl.ds(s * 256, 256)], cast_r.at[s])
 
     def left_product(j):
         part = lax.dot_general(lh[j], gz[...], (((0,), (0,)), ((), ())), preferred_element_type=F32).astype(BF)
@@ -256,7 +261,7 @@
     def right_product(j):
         lr_sum.ready(j)
         rp[j] = jnp.dot(
-            lr[j].reshape(512, 1024), rr[...], preferred_element_type=F32
+            lr[j].reshape(512, 1024), rr[...].reshape(1024, 512), preferred_element_type=F32
         ).astype(BF).reshape(4, 2, 64, 512)
         rot_rs.start(j)
 
@@ -274,145 +279,172 @@
             dx[j, x, h] = (first_new / (jnp.sqrt(second_new) + 1e-08)).astype(BF)
         d_ag.start(j)
 
-    def right_back(j):
-        d_ag.end(j)
-
+    def right_back(p, j):
+        if j not in waited:
+            waited.append(j)
+            d_ag.end(j)
         part = lax.dot_general(
-            dx[j].reshape(512, 512), rr[...], (((1,), (1,)), ((), ())), preferred_element_type=F32
+            dx[j].reshape(512, 512), rr[:, p].reshape(512, 512), (((1,), (1,)), ((), ())), preferred_element_type=F32
         ).astype(BF)
         for t in range(4):
-            ep[j, t] = part[:, t * 256 : t * 256 + 256].reshape(4, 2, 64, 256)
-        e_sum.swap(j)
-
-    def left_back(k):
+            ep[p * NJ + j, t] = part[:, t * 128 : t * 128 + 128].reshape(4, 2, 64, 128)
+        e_sum.swap(p * NJ + j)
+
+    def left_back(p, k):
         rows = pl.ds(k * KC, KC)
-
-        total = jnp.dot(lh[0, rows], ee[0].reshape(512, 1024), preferred_element_type=F32)
+        total = jnp.dot(lh[0, rows], ee[p * NJ].reshape(512, 512), preferred_element_type=F32)
         for j in range(1, NJ):
-            total = total + jnp.dot(lh[j, rows], ee[j].reshape(512, 1024), preferred_element_type=F32)
+            total = total + jnp.dot(lh[j, rows], ee[p * NJ + j].reshape(512, 512), preferred_element_type=F32)
         for t in range(4):
-            up[t, rows] = total[:, t * 256 : t * 256 + 256].astype(BF)
-        u_rs.start(k)
-
-    def last(k):
-        u_rs.end(k)
-        rows = pl.ds(k * KC, KC)
-        outs.append(local(u_out.at[rows], u_ref.at[rows], 4 + k))
-
+            up[p, t, rows] = total[:, t * 128 : t * 128 + 128].astype(BF)
+        u_rs.start(p * NK + k)
+
+    def last(j):
+        u_rs.end(j)
+        here = (pl.ds(j % NK * KC, KC), pl.ds(j // NK * 128, 128))
+        outs.append(local(u_out.at[here], u_ref.at[here], 4 + j))
+
+    waited = []
     l_ag.start(0)
-    l_ag.start(1)
     g_ag.start(0)
     own = [local(g_ref, gz.at[:, block(z, 256)], 1)]
     for j in range(4):
         own.append(local(l_ref.at[:, pl.ds(j * 128, 128)], lh.at[j, :, block(x, 128)], 4 + j))
     moments = [local(fm_ref, fm, 2), local(sm_ref, sm, 3)]
-    g_ag.mid(0)
+    l_ag.start(1)
     g_ag.start(1)
     g_ag.start(2)
     g_ag.start(3)
+    g_ag.mid(0)
     l_ag.mid(0)
     g_ag.mid(1)
+    g_ag.mid(2)
     l_ag.mid(1)
-    g_ag.mid(2)
+    g_ag.mid(3)
     right_send()
     l_ag.start(2)
     l_ag.start(3)
-    g_ag.mid(3)
     for copy in own:
         copy.wait()
-    l_ag.end(1)
+    l_ag.end(0)
     g_ag.end(0)
     g_ag.end(1)
     g_ag.end(2)
     g_ag.end(3)
+    left_product(0)
+    lr_sum.add(0)
+    l_ag.end(1)
     left_product(1)
+    lr_rs.mid(0)
+    right_cast()
     lr_sum.add(1)
-    l_ag.end(0)
-    left_product(0)
-    right_cast()
     lr_rs.mid(1)
-    lr_sum.add(0)
+    lr_sum.turn(0)
+    l_ag.mid(3)
+    lr_ag.mid(0)
     lr_sum.turn(1)
-    lr_rs.mid(0)
-    l_ag.mid(3)
     l_ag.mid(2)
-    lr_ag.mid(1)
-    lr_sum.turn(0)
-    lr_sum.end(1)
+    lr_sum.end(0)
     l_ag.end(3)
     left_product(3)
+    lr_ag.mid(1)
     right_ready()
-    right_product(1)
-    lr_ag.mid(0)
+    right_product(0)
     l_ag.end(2)
     left_product(2)
     lr_sum.add(3)
-    rot_rs.mid(1)
-    lr_sum.end(0)
-    right_product(0)
+    lr_sum.end(1)
+    rot_rs.mid(0)
+    lr_sum.add(2)
+    right_product(1)
     lr_rs.mid(3)
-    lr_sum.add(2)
     for copy in moments:
         copy.wait()
+    moment_step(0)
+    lr_rs.mid(2)
+    rot_rs.mid(1)
+    lr_sum.turn(3)
+    lr_ag.mid(3)
     moment_step(1)
-    rot_rs.mid(0)
-    lr_sum.turn(3)
-    lr_rs.mid(2)
+    lr_sum.turn(2)
+    d_ag.mid(0)
     d_ag.mid(1)
-    lr_ag.mid(3)
-    moment_step(0)
-    lr_sum.turn(2)
-    right_back(1)
     lr_sum.end(3)
-    d_ag.mid(0)
     lr_ag.mid(2)
+    right_product(3)
+    right_back(0, 0)
+    right_back(0, 1)
+    lr_sum.end(2)
+    right_back(1, 1)
+    e_sum.add(0)
     e_sum.add(1)
-    right_product(3)
-    lr_sum.end(2)
-    right_back(0)
     rot_rs.mid(3)
     right_product(2)
-    e_sum.add(0)
+    e_rs.mid(0)
+    e_sum.add(5)
+    right_back(1, 0)
+    e_rs.mid(1)
     moment_step(3)
+    e_sum.add(4)
+    e_sum.turn(0)
     rot_rs.mid(2)
-    e_rs.mid(1)
-    e_rs.mid(0)
+    e_rs.mid(5)
+    e_sum.turn(1)
+    e_rs.mid(4)
     d_ag.mid(3)
-    e_sum.turn(1)
+    e_ag.mid(0)
     moment_step(2)
     outs += [local(fm, fn_ref, 2), local(sm, sn_ref, 3)]
-    e_sum.turn(0)
-    right_back(3)
+    e_sum.turn(5)
     e_ag.mid(1)
+    right_back(0, 3)
+    e_sum.turn(4)
+    right_back(1, 3)
+    e_sum.end(0)
+    e_sum.add(3)
+    e_ag.mid(5)
     d_ag.mid(2)
-    e_sum.add(3)
-    e_ag.mid(0)
-    right_back(2)
+    e_sum.add(7)
+    e_sum.end(1)
+    e_ag.mid(4)
     e_rs.mid(3)
+    right_back(0, 2)
+    right_back(1, 2)
+    e_sum.end(5)
+    e_rs.mid(7)
     e_sum.add(2)
-    e_sum.end(0)
+    e_sum.turn(3)
     e_rs.mid(2)
-    e_sum.turn(3)
-    e_sum.end(1)
+    e_sum.add(6)
+    e_ag.mid(3)
     e_sum.turn(2)
-    e_ag.mid(3)
+    e_rs.mid(6)
     e_ag.mid(2)
     e_sum.end(3)
+    e_sum.turn(7)
+    e_sum.end(4)
+    e_sum.turn(6)
     e_sum.end(2)
-    for j in range(NJ):
+    for j in range(0, 4):
         e_sum.ready(j)
-    left_back(1)
-    left_back(3)
-    left_back(0)
+    left_back(0, 1)
+    e_ag.mid(6)
+    e_ag.mid(7)
+    left_back(0, 0)
+    e_sum.end(6)
     u_rs.mid(1)
-    left_back(2)
+    e_sum.end(7)
+    for j in range(4, 8):
+        e_sum.ready(j)
+    left_back(1, 0)
+    u_rs.mid(0)
+    left_back(1, 1)
+    u_rs.mid(2)
     u_rs.mid(3)
-    u_rs.mid(0)
+    last(0)
     last(1)
-    u_rs.mid(2)
+    last(2)
     last(3)
-    last(0)
-    last(2)
     for copy in outs:
         copy.wait()
 
@@ -441,24 +473,24 @@
     scratch = [
         pltpu.VMEM((1024, 1024), BF),
         pltpu.VMEM((NJ, 1024, 512), BF),
-        pltpu.VMEM((1024, 512), BF),
+        pltpu.VMEM((4, 2, 128, 512), BF),
         pltpu.VMEM((NJ, 4, 4, 2, 64, 256), BF),
         pltpu.VMEM((NJ, 4, 4, 64, 256), BF),
         pltpu.VMEM((NJ, 4, 2, 64, 1024), BF),
         pltpu.VMEM((NJ, 4, 2, 64, 512), BF),
         pltpu.VMEM((512, 512), BF),
         pltpu.VMEM((NJ, 4, 2, 64, 512), BF),
-        pltpu.VMEM((NJ, 4, 4, 2, 64, 256), BF),
-        pltpu.VMEM((NJ, 4, 4, 64, 256), BF),
-        pltpu.VMEM((NJ, 4, 2, 64, 1024), BF),
-        pltpu.VMEM((4, 1024, 256), BF),
+        pltpu.VMEM((NP * NJ, 4, 4, 2, 64, 128), BF),
+        pltpu.VMEM((NP * NJ, 4, 4, 64, 128), BF),
+        pltpu.VMEM((NP * NJ, 4, 2, 64, 512), BF),
+        pltpu.VMEM((NP, 4, 1024, 128), BF),
         pltpu.VMEM((1024, 256), BF),
         pltpu.VMEM((512, 512), F32),
         pltpu.VMEM((512, 512), F32),
     ]
-    for chunks, half in ((NJ, (2, 64, 256)), (NJ, (64, 512)), (NJ, (2, 64, 256)), (NK, (KC // 2, 256))):
+    for chunks, half in ((NJ, (2, 64, 256)), (NJ, (64, 512)), (NP * NJ, (2, 64, 128)), (NP * NK, (KC // 2, 128))):
         scratch += scatter_buffers(chunks, half)
-    scratch += [dma((n,)) for n in (11, 3 * (NG + 7 * NJ + NK), 4 * NJ, 1, 2, 3, 2, 8)]
+    scratch += [dma((n,)) for n in (11, 2 * (NG + 5 * NJ + 2 * NP * NJ + NP * NK), 2 * (1 + NP) * NJ, 1, 2, 3, 2, 8)]
     anywhere = pl.BlockSpec(memory_space=pl.ANY)
     results = pl.pallas_call(
         kernel,
@@ -474,7 +506,7 @@
             collective_id=0, has_side_effects=True, vmem_limit_bytes=60 * 1024 * 1024
         ),
         cost_estimate=pl.CostEstimate(flops=12884901888, bytes_accessed=6553600, transcendentals=262144),
-    )(grad, basis_left, basis_right, first_moment, second_moment)
+    )(grad, basis_left, basis_right.reshape(2, 2, 128, 256), first_moment, second_moment)
 
     def hand_over(u, fn, sn, u_out, fn_out, sn_out, u_held, fn_held, sn_held, sems):
         steps = []

time: 146 us -> 144 us (0.986); the launches traced: 145 us -> 144 us
  no operation moved by 1% of the time
where the time goes in v5:
time: 144 us
  Pallas kernels  143 us (99%)
    pallas_call x1, Pallas kernels, per_device(): pl.pallas_call(kernel, out_shape=(jax.ShapeDtypeStruct((1024, 256), BF),...  141 us

profile of v5, /device:TPU:0, one launch (start us, length us, event | category | flops | bytes accessed | tf_op | source)
XLA Modules:
  0.0 144.2 jit_solution(14058562991136636242)
XLA Ops:
  0.6 140.8 %shard_map.76 = (bf16[1024,256]{1,0:T(8,128)(2,1)}, f32[512,512]{1,0:T(8,128)}, f32[512,512]{1,0:T(8,128)}) custom-call(bf16[1024,256]{1,0:T(8,128)(2,1)} %g_ref.1, bf16[1024,512]{1,0:T(8,128)(2,1)} %l_ref.1, bf16[2,2,128,256]{3,2,1,0:T(8,128)(2,1)} %bitcast.1, f32[512,512]{1,0:T(8,128)} %fm_ref.1, f32[512,512]{1,0:T(8,128)} %sm_ref.1), custom_call_target="tpu_custom_call" | custom-call | flops 12884901888 | bytes 6553600 | tf_op jit(solution)/shard_map/pallas_call | solution.py:495
  141.5 2.6 %shard_map.77 = (bf16[1024,256]{1,0:T(8,128)(2,1)}, f32[512,512]{1,0:T(8,128)}, f32[512,512]{1,0:T(8,128)}) custom-call(bf16[1024,256]{1,0:T(8,128)(2,1)} %get-tuple-element.6.u, f32[512,512]{1,0:T(8,128)} %get-tuple-element.7.fn, f32[512,512]{1,0:T(8,128)} %get-tuple-element.8.sn), custom_call_target="tpu_custom_call" | custom-call | bytes 5242880 | tf_op jit(solution)/shard_map/pallas_call | solution.py:528

commit v6 on v5

--- a/solution.py
+++ b/solution.py
@@ -311,19 +311,19 @@
     for j in range(4):
         own.append(local(l_ref.at[:, pl.ds(j * 128, 128)], lh.at[j, :, block(x, 128)], 4 + j))
     moments = [local(fm_ref, fm, 2), local(sm_ref, sm, 3)]
-    l_ag.start(1)
     g_ag.start(1)
     g_ag.start(2)
-    g_ag.start(3)
+    l_ag.start(1)
     g_ag.mid(0)
     l_ag.mid(0)
     g_ag.mid(1)
     g_ag.mid(2)
     l_ag.mid(1)
-    g_ag.mid(3)
     right_send()
+    g_ag.start(3)
     l_ag.start(2)
     l_ag.start(3)
+    g_ag.mid(3)
     for copy in own:
         copy.wait()
     l_ag.end(0)
@@ -332,119 +332,119 @@
     g_ag.end(2)
     g_ag.end(3)
     left_product(0)
-    lr_sum.add(0)
     l_ag.end(1)
     left_product(1)
+    lr_sum.add(0)
+    lr_sum.add(1)
+    right_cast()
     lr_rs.mid(0)
-    right_cast()
-    lr_sum.add(1)
+    l_ag.mid(2)
     lr_rs.mid(1)
     lr_sum.turn(0)
     l_ag.mid(3)
+    lr_sum.turn(1)
     lr_ag.mid(0)
-    lr_sum.turn(1)
-    l_ag.mid(2)
+    lr_ag.mid(1)
+    l_ag.end(2)
+    left_product(2)
     lr_sum.end(0)
+    lr_sum.end(1)
+    lr_sum.add(2)
+    right_ready()
+    right_product(0)
+    right_product(1)
     l_ag.end(3)
     left_product(3)
-    lr_ag.mid(1)
-    right_ready()
-    right_product(0)
-    l_ag.end(2)
-    left_product(2)
+    lr_rs.mid(2)
+    rot_rs.mid(0)
     lr_sum.add(3)
-    lr_sum.end(1)
-    rot_rs.mid(0)
-    lr_sum.add(2)
-    right_product(1)
+    lr_sum.turn(2)
+    rot_rs.mid(1)
     lr_rs.mid(3)
     for copy in moments:
         copy.wait()
     moment_step(0)
-    lr_rs.mid(2)
-    rot_rs.mid(1)
+    moment_step(1)
+    lr_ag.mid(2)
+    d_ag.mid(0)
     lr_sum.turn(3)
+    lr_sum.end(2)
+    d_ag.mid(1)
+    right_product(2)
     lr_ag.mid(3)
-    moment_step(1)
-    lr_sum.turn(2)
-    d_ag.mid(0)
-    d_ag.mid(1)
-    lr_sum.end(3)
-    lr_ag.mid(2)
-    right_product(3)
     right_back(0, 0)
     right_back(0, 1)
-    lr_sum.end(2)
     right_back(1, 1)
+    e_sum.add(1)
+    rot_rs.mid(2)
+    lr_sum.end(3)
+    right_product(3)
+    e_rs.mid(1)
     e_sum.add(0)
-    e_sum.add(1)
+    e_sum.add(5)
+    moment_step(2)
+    right_back(1, 0)
+    e_sum.turn(1)
+    e_sum.add(4)
     rot_rs.mid(3)
-    right_product(2)
     e_rs.mid(0)
-    e_sum.add(5)
-    right_back(1, 0)
-    e_rs.mid(1)
+    e_rs.mid(5)
+    e_ag.mid(1)
+    d_ag.mid(2)
+    e_rs.mid(4)
     moment_step(3)
-    e_sum.add(4)
+    outs += [local(fm, fn_ref, 2), local(sm, sn_ref, 3)]
     e_sum.turn(0)
-    rot_rs.mid(2)
-    e_rs.mid(5)
-    e_sum.turn(1)
-    e_rs.mid(4)
+    e_sum.turn(5)
+    right_back(0, 2)
+    e_sum.turn(4)
     d_ag.mid(3)
     e_ag.mid(0)
-    moment_step(2)
-    outs += [local(fm, fn_ref, 2), local(sm, sn_ref, 3)]
-    e_sum.turn(5)
-    e_ag.mid(1)
+    e_sum.add(2)
+    e_ag.mid(5)
+    right_back(1, 2)
+    e_ag.mid(4)
+    e_sum.add(6)
+    e_sum.end(0)
     right_back(0, 3)
-    e_sum.turn(4)
+    e_sum.add(3)
+    e_sum.end(5)
+    e_sum.end(4)
+    e_rs.mid(2)
+    e_sum.end(1)
+    e_rs.mid(6)
     right_back(1, 3)
-    e_sum.end(0)
-    e_sum.add(3)
-    e_ag.mid(5)
-    d_ag.mid(2)
+    e_rs.mid(3)
     e_sum.add(7)
-    e_sum.end(1)
-    e_ag.mid(4)
-    e_rs.mid(3)
-    right_back(0, 2)
-    right_back(1, 2)
-    e_sum.end(5)
+    e_sum.turn(2)
+    e_sum.turn(3)
+    e_ag.mid(2)
     e_rs.mid(7)
-    e_sum.add(2)
-    e_sum.turn(3)
-    e_rs.mid(2)
-    e_sum.add(6)
     e_ag.mid(3)
-    e_sum.turn(2)
-    e_rs.mid(6)
-    e_ag.mid(2)
-    e_sum.end(3)
-    e_sum.turn(7)
-    e_sum.end(4)
     e_sum.turn(6)
     e_sum.end(2)
+    e_sum.turn(7)
+    e_sum.end(3)
+    e_ag.mid(6)
     for j in range(0, 4):
         e_sum.ready(j)
+    left_back(0, 0)
+    e_ag.mid(7)
     left_back(0, 1)
-    e_ag.mid(6)
-    e_ag.mid(7)
-    left_back(0, 0)
+    e_sum.end(7)
+    u_rs.mid(0)
     e_sum.end(6)
-    u_rs.mid(1)
-    e_sum.end(7)
     for j in range(4, 8):
         e_sum.ready(j)
+    left_back(1, 1)
+    u_rs.mid(1)
     left_back(1, 0)
-    u_rs.mid(0)
-    left_back(1, 1)
+    last(0)
+    u_rs.mid(3)
+    last(1)
     u_rs.mid(2)
-    u_rs.mid(3)
-    last(0)
-    last(1)
+    last(3)
     last(2)
-    last(3)
     for copy in outs:
         copy.wait()
 

time: 144 us -> 144 us (level)
  no operation moved by 1% of the time
where the time goes in v6:
time: 144 us; the launch traced here: 143 us
  Pallas kernels  142 us (99%)
    pallas_call x1, Pallas kernels, per_device(): pl.pallas_call(kernel, out_shape=(jax.ShapeDtypeStruct((1024, 256), BF),...  140 us

profile of v6, /device:TPU:0, one launch (start us, length us, event | category | flops | bytes accessed | tf_op | source)
XLA Modules:
  0.0 143.3 jit_solution(13412582178156426724)
XLA Ops:
  0.6 139.9 %shard_map.76 = (bf16[1024,256]{1,0:T(8,128)(2,1)}, f32[512,512]{1,0:T(8,128)}, f32[512,512]{1,0:T(8,128)}) custom-call(bf16[1024,256]{1,0:T(8,128)(2,1)} %g_ref.1, bf16[1024,512]{1,0:T(8,128)(2,1)} %l_ref.1, bf16[2,2,128,256]{3,2,1,0:T(8,128)(2,1)} %bitcast.1, f32[512,512]{1,0:T(8,128)} %fm_ref.1, f32[512,512]{1,0:T(8,128)} %sm_ref.1), custom_call_target="tpu_custom_call" | custom-call | flops 12884901888 | bytes 6553600 | tf_op jit(solution)/shard_map/pallas_call | solution.py:495
  140.6 2.6 %shard_map.77 = (bf16[1024,256]{1,0:T(8,128)(2,1)}, f32[512,512]{1,0:T(8,128)}, f32[512,512]{1,0:T(8,128)}) custom-call(bf16[1024,256]{1,0:T(8,128)(2,1)} %get-tuple-element.6.u, f32[512,512]{1,0:T(8,128)} %get-tuple-element.7.fn, f32[512,512]{1,0:T(8,128)} %get-tuple-element.8.sn), custom_call_target="tpu_custom_call" | custom-call | bytes 5242880 | tf_op jit(solution)/shard_map/pallas_call | solution.py:528
